TPU v7x, 512 devices: a whole 4x4x16 slice. The times are simulated.
512 devices in a mesh: gen: 2 (over z_hi), row: 64 (over z_lo, x, core), col: 4 (over y).
Axes of the slice: x: 4, y: 4, z: 16 (z_hi: 2, z_lo: 8; z = z_hi * 8 + z_lo), core: 2. Of those that a mesh axis runs over, the one named last changes fastest.
Arguments:
- coords: int32 [2, 65536], P(None, 'row'), may hold values from 0 to 1023
- factor: float32 [65536, 8192], P('row', ('gen', 'col')), as said below
Outputs:
- panel_factor: float32 [65536, 512], P('row', ('gen', 'col'))
Inputs may be any that keep to these rules, and one draw needn't show every extreme that they name: `factor`: the kernel at the panel's points minus panel_rows panel_rows^T is positive definite.
All inputs are finite; a program needn't handle non-finite values.
Results may differ from a plain program's by a relative error of at most 0.0003.
Values sent between devices are 32-bit elements; how exact they have to be, the bound alone decides.
A program may use at most 64 MiB of HBM per device.

v0:
```python
import jax
import jax.numpy as jnp
from jax import lax
from jax.sharding import PartitionSpec as P

B = 512
GRID = 1024


root_three = 1.7320508075688772
length_scale = 0.2
nugget_term = 1.0


def panel_kernel(row_points, col_points, row_ids, col_ids):
    delta_x = row_points[0][:, None] - col_points[0][None, :]
    delta_y = row_points[1][:, None] - col_points[1][None, :]
    scaled = root_three * jnp.sqrt(delta_x * delta_x + delta_y * delta_y) / length_scale
    same = jnp.where(
        row_ids[:, None] == col_ids[None, :], jnp.float32(nugget_term), jnp.float32(0.0)
    )
    return (1.0 + scaled) * jnp.exp(-scaled) + same


def solve_rows(lower, block):
    return lax.linalg.triangular_solve(lower, block, left_side=False, lower=True, transpose_a=True)


def shards(coords, factor):
    rows = factor.shape[0]
    groups = lax.axis_size(("gen", "col"))
    panel_width = B
    panel_here = panel_width // lax.axis_size("row")
    slice_width = panel_width // groups
    points = coords.astype(jnp.float32) / GRID
    panel_rows, panel_points = (
        lax.all_gather(factor[:panel_here], "row", axis=0, tiled=True),
        lax.all_gather(points[:, :panel_here], "row", axis=1, tiled=True),
    )
    update = lax.dot_general(
        factor,
        panel_rows,
        (((1,), (1,)), ((), ())),
        precision=lax.Precision.HIGHEST,
        preferred_element_type=jnp.float32,
    )
    row_ids = lax.axis_index("row") * rows + jnp.arange(rows, dtype=jnp.int32)
    columns = jnp.arange(panel_width, dtype=jnp.int32)
    col_ids = columns // panel_here * rows + columns % panel_here
    start = lax.axis_index(("gen", "col")) * slice_width
    slice_points = lax.dynamic_slice_in_dim(panel_points, start, slice_width, 1)
    slice_ids = lax.dynamic_slice_in_dim(col_ids, start, slice_width, 0)
    shares = lax.psum_scatter(update, ("gen", "col"), scatter_dimension=1, tiled=True)
    updated_slice = panel_kernel(points, slice_points, row_ids, slice_ids) - shares
    updated = lax.all_gather(updated_slice, ("gen", "col"), axis=1, tiled=True)
    top_rows = updated[:panel_here]
    diagonal_block = lax.all_gather(top_rows, "row", axis=0, tiled=True)
    lower = jnp.linalg.cholesky(diagonal_block)
    solved = solve_rows(lower, updated)
    return lax.dynamic_slice_in_dim(solved, start, slice_width, 1)


def solution(mesh):
    in_specs = (P(None, "row"), P("row", ("gen", "col")))
    out_specs = P("row", ("gen", "col"))
    return jax.shard_map(shards, mesh=mesh, in_specs=in_specs, out_specs=out_specs, check_vma=False)
```

profile of v0, /device:TPU:1, one launch (start us, length us, event | category | flops | bytes accessed | tf_op | source)
XLA Modules:
  0.0 665.5 jit_solution(6483349254199363993)
XLA Ops:
  6.5 1.4 slice.129
  8.0 127.9 %all-gather.5.cloned.1.call-done = f32[512,1024]{1,0:T(8,128)} async-done(((f32[8,1024]{1,0:T(8,128)}), f32[512,1024]{1,0:T(8,128)}) %all-gather.5.cloned.1.call-update) | async-done | bytes 2097168 | tf_op jit(solution)/shard_map/all_gather | solution.py:37
  135.9 10.2 %fusion.49 = f32[1024,512]{0,1:T(8,128)} fusion(f32[1024,1024]{1,0:T(8,128)} %param.3, f32[512,1024]{1,0:T(8,128)} %all-gather.5.cloned.1.call-done), kind=kOutput, calls=%fused_computation.96 | convolution fusion | flops 6442450944 | bytes 8388608 | tf_op jit(solution)/shard_map/dot_general | solution.py:40
  146.2 0.6 copy-done.1
  146.9 122.0 %all-gather = f32[64,8,2]{1,2,0:T(2,128)S(1)} all-gather(f32[1,8,2]{1,2,0:T(2,128)S(1)} %slice_bitcast_fusion.8), channel_id=1, replica_groups=mesh['gen'=2,'row'=64,'col'=4] {'row'}, dimensions={0}, use_global_device_ids=true | all-gather | bytes 4160 | tf_op jit(solution)/shard_map/all_gather | solution.py:38
  269.1 18.0 %reduce-scatter.2.cloned.1.call-done = f32[1024,64]{0,1:T(8,128)} async-done(((f32[1024,512]{0,1:T(8,128)}), f32[1024,64]{0,1:T(8,128)}) %reduce-scatter.2.cloned.1.call-update) | async-done | bytes 262160 | tf_op jit(solution)/shard_map/reduce_scatter | solution.py:53
  287.1 1.9 add_subtract_fusion
  289.0 0.5 all-gather.9.cloned.1.call-start
  289.5 110.2 %all-gather.7.cloned.1.call-done = f32[1024,512]{0,1:T(8,128)} async-done(((f32[1024,64]{0,1:T(8,128)}), f32[1024,512]{0,1:T(8,128)}) %all-gather.7.cloned.1.call-update) | async-done | bytes 2097168 | tf_op jit(solution)/shard_map/all_gather | solution.py:55
  399.7 1.0 slice.145
  400.7 0.7 copy.7
  401.5 114.6 %all-gather.9.cloned.1.call-done = f32[512,512]{1,0:T(8,128)} async-done(((f32[8,512]{1,0:T(8,128)}), f32[512,512]{1,0:T(8,128)}) %all-gather.9.cloned.1.call-update) | async-done | bytes 1048592 | tf_op jit(solution)/shard_map/all_gather | solution.py:57
  516.1 1.6 copy.8
  517.8 0.2 fusion.12
  518.0 11.7 %cholesky.104 = f32[128,128]{1,0:T(8,128)S(1)} custom-call(f32[128,128]{1,0:T(8,128)S(1)} %cholesky.266), custom_call_target="Cholesky" | custom-call | tf_op jit(solution)/shard_map/jit(cholesky)/cholesky | solution.py:58
  529.9 9.8 %custom-call.30 = f32[1,128,128]{1,2,0:T(8,128)S(1)} custom-call(f32[1,128,128]{2,1,0:T(8,128)S(1)} %get-tuple-element.32), custom_call_target="InvertDiagBlocksLowerTriangular" | custom-call | tf_op jit(solution)/shard_map/jit(cholesky)/cholesky | solution.py:58
  539.7 0.3 constant_dynamic-update-slice_fusion
  540.0 0.3 convolution_subtract_fusion.2
  540.4 11.7 %cholesky.217 = f32[128,128]{1,0:T(8,128)S(1)} custom-call(f32[128,128]{1,0:T(8,128)S(1)} %cholesky.270), custom_call_target="Cholesky" | custom-call | tf_op jit(solution)/shard_map/jit(cholesky)/cholesky | solution.py:58
  552.1 10.0 %custom-call.31 = f32[1,128,128]{1,2,0:T(8,128)S(1)} custom-call(f32[1,128,128]{2,1,0:T(8,128)S(1)} %get-tuple-element.29), custom_call_target="InvertDiagBlocksLowerTriangular" | custom-call | tf_op jit(solution)/shard_map/jit(cholesky)/cholesky | solution.py:58
  562.1 0.3 convolution_dynamic-update-slice_fusion
  562.4 0.4 convolution_subtract_fusion.3
  562.8 11.7 %cholesky.238 = f32[128,128]{1,0:T(8,128)S(1)} custom-call(f32[128,128]{1,0:T(8,128)S(1)} %cholesky.275), custom_call_target="Cholesky" | custom-call | tf_op jit(solution)/shard_map/jit(cholesky)/cholesky | solution.py:58
  574.5 0.7 compare_reduce_fusion.1
  575.2 9.8 %custom-call.32 = f32[1,128,128]{1,2,0:T(8,128)S(1)} custom-call(f32[1,128,128]{2,1,0:T(8,128)S(1)} %get-tuple-element.26), custom_call_target="InvertDiagBlocksLowerTriangular" | custom-call | tf_op jit(solution)/shard_map/jit(cholesky)/cholesky | solution.py:58
  585.0 0.2 convolution_dynamic-update-slice_fusion.1
  585.2 0.4 convolution_subtract_fusion.4
  585.6 11.7 %cholesky.255 = f32[128,128]{1,0:T(8,128)S(1)} custom-call(f32[128,128]{1,0:T(8,128)S(1)} %convolution_subtract_fusion.4), custom_call_target="Cholesky" | custom-call | tf_op jit(solution)/shard_map/jit(cholesky)/cholesky | solution.py:58
  597.3 0.7 compare_reduce_fusion
  598.0 0.9 compare_reduce_fusion.2
  601.5 7.9 %while.1 = (s32[]{:T(128)}, f32[512,512]{1,0:T(8,128)S(1)}, s32[4,2]{0,1:T(2,128)S(1)}, f32[4,128,128]{2,1,0:T(8,128)S(1)}, s32[]{:T(128)}) while((s32[]{:T(128)}, f32[512,512]{1,0:T(8,128)S(1)}, s32[4,2]{0,1:T(2,128)S(1)}, f32[4,128,128]{2,1,0:T(8,128)S(1)}, s32[]{:T(128)}) %tuple.29), condition=%wide.while_cond, body=%wide.while_body.sunk | while | flops 2 | bytes 131181 | solution.py:26
  601.6 0.5 fusion.58
  602.1 1.4 bitcast_dynamic-update-slice_fusion.2
  603.6 0.5 fusion.58
  604.1 1.4 bitcast_dynamic-update-slice_fusion.2
  605.5 0.5 fusion.58
  606.1 1.4 bitcast_dynamic-update-slice_fusion.2
  607.5 0.5 fusion.58
  608.0 1.4 bitcast_dynamic-update-slice_fusion.2
  609.4 39.3 %custom-call.33 = f32[4,128,128]{1,2,0:T(8,128)S(1)} custom-call(f32[4,128,128]{2,1,0:T(8,128)S(1)} %get-tuple-element.12), custom_call_target="InvertDiagBlocksLowerTriangular" | custom-call | tf_op jit(solution)/shard_map/triangular_solve | solution.py:26
  648.7 1.7 fusion.13
  650.4 1.7 convolution_subtract_fusion.1
  652.0 0.6 fusion.28
  652.7 1.8 convolution_subtract_fusion
  654.4 0.6 fusion.27
  655.0 2.2 fusion.6
  657.3 0.6 fusion.26
  657.9 0.8 fusion.17
  (36 shorter events, 1.2 us)
Async XLA Ops:
  6.5 129.4 %all-gather.5.cloned.1.call-start = ((), (), s32[]{:S(2)}) async-start(), calls=%async_computation.1 | async-start | bytes 2129920 | tf_op jit(solution)/shard_map/all_gather | solution.py:37
  7.9 279.1 %reduce-scatter.2.cloned.1.call-start = ((), (), s32[]{:S(2)}) async-start(), calls=%async_computation.2 | async-start | bytes 2359296 | tf_op jit(solution)/shard_map/reduce_scatter | solution.py:53
  146.1 0.7 copy-start.1
  146.2 253.6 %all-gather.7.cloned.1.call-start = ((), (), s32[]{:S(2)}) async-start(), calls=%async_computation.3 | async-start | bytes 2359296 | tf_op jit(solution)/shard_map/all_gather | solution.py:55
  289.0 227.1 %all-gather.9.cloned.1.call-start = ((), (), s32[]{:S(2)}) async-start(), calls=%async_computation.4 | async-start | bytes 1064960 | tf_op jit(solution)/shard_map/all_gather | solution.py:57
  516.1 1.7 copy-start
Sparse Core Ops, SparseCore 0:
  9.5 126.3 all-gather.4
  146.3 140.7 reduce-scatter.1
  290.8 108.9 all-gather.6
  402.0 114.0 all-gather.8
where the time goes:
time: 670 us; the launch traced here: 665 us
  waiting for transfers between devices  371 us (55%)
  blocking collectives  122 us (18%)
  other arithmetic  121 us (18%)
  matrix products  21.2 us (3%)
  between operations  16.1 us (2%)
  local copies, waits for them, and re-layouts  13.5 us (2%)
    all_gather x1, waiting for transfers between devices, shards(): lax.all_gather(factor[:panel_here], 'row', axis=0, tiled=True)  128 us
    all_gather x1, blocking collectives, shards(): lax.all_gather(points[:, :panel_here], 'row', axis=1, tiled=True)  122 us
    all_gather x1, waiting for transfers between devices, shards(): diagonal_block = lax.all_gather(top_rows, 'row', axis=0, tiled=True)  115 us
    all_gather x1, waiting for transfers between devices, shards(): updated = lax.all_gather(updated_slice, ('gen', 'col'), axis=1, tiled=True)  110 us
    another operation x14, other arithmetic, shards(): lower = jnp.linalg.cholesky(diagonal_block)  78.7 us
    another operation x4, other arithmetic, solve_rows(): lax.linalg.triangular_solve(lower, block, left_side=False, lower=True, tr...  40.3 us
    reduce_scatter x1, waiting for transfers between devices, shards(): lax.psum_scatter(update, ('gen', 'col'), scatter_dimension=1, tiled=True)  18 us
  transfers between devices with their start and end apart: 4, of which 4 were waited for; matrix products, arithmetic and copies ran while one was open for 0% of the time, Pallas kernels for 0%

commit v1 on v0

v1 whole, which is shorter than its diff:
```python
import jax
import jax.numpy as jnp
from jax import lax
from jax.experimental import pallas as pl
from jax.experimental.pallas import tpu as pltpu
from jax.sharding import PartitionSpec as P

B = 512
GRID = 1024
PAN = 8
ROWS = 1024
DEPTH = 1024
QUART = 256
NZ, NX, NC, NCOL = 8, 4, 2, 4
WIDE = DEPTH + 128

root_three = 1.7320508075688772
length_scale = 0.2
nugget_term = 1.0

HI = lax.Precision.HIGHEST
MESH = pl.DeviceIdType.MESH


def dotf(a, b, dims):
    return lax.dot_general(a, b, (dims, ((), ())), precision=HI, preferred_element_type=jnp.float32)


def matern(delta_x, delta_y):
    scaled = root_three * jnp.sqrt(delta_x * delta_x + delta_y * delta_y) / length_scale
    return (1.0 + scaled) * jnp.exp(-scaled)


def spread(x, k):
    return jnp.broadcast_to(x[k : k + 1], x.shape)


def inverse_factor(tile_ref, out_ref):
    sub = lax.broadcasted_iota(jnp.int32, (8, 128), 0)
    lane = lax.broadcasted_iota(jnp.int32, (8, 128), 1)
    a = [tile_ref[8 * i : 8 * i + 8, :] for i in range(16)]
    t = [jnp.where(lane == sub + 8 * i, jnp.float32(1), jnp.float32(0)) for i in range(16)]
    for b in range(16):
        cols = [jnp.broadcast_to(a[b][:, 8 * b + k : 8 * b + k + 1], (8, 128)) for k in range(8)]
        recip, cross, scale = [], [], jnp.ones((8, 128), jnp.float32)
        for k in range(8):
            pivot = spread(cols[k], k)
            r = 1.0 / pivot
            recip.append(r)
            scale = jnp.where(sub == k, pivot, scale)
            m = jnp.where(sub > k, cols[k] * r, 0.0)
            row = []
            for j in range(k + 1, 8):
                s = spread(cols[j], k)
                row.append(s)
                cols[j] = cols[j] - m * s
            cross.append(row)
            a[b] = a[b] - m * spread(a[b], k)
            t[b] = t[b] - m * spread(t[b], k)
        ua = [spread(a[b], k) for k in range(8)]
        ut = [spread(t[b], k) for k in range(8)]
        out_ref[8 * b : 8 * b + 8, :] = t[b] * lax.rsqrt(scale)
        for i in range(b + 1, 16):
            c = [jnp.broadcast_to(a[i][:, 8 * b + k : 8 * b + k + 1], (8, 128)) for k in range(8)]
            da = dt = None
            for k in range(8):
                m = c[k] * recip[k]
                for j in range(k + 1, 8):
                    c[j] = c[j] - m * cross[k][j - k - 1]
                da = m * ua[k] if da is None else da + m * ua[k]
                dt = m * ut[k] if dt is None else dt + m * ut[k]
            a[i] = a[i] - da
            t[i] = t[i] - dt


def place():
    h, r, c = lax.axis_index("gen"), lax.axis_index("row"), lax.axis_index("col")
    return h, r, c, r // 8, (r // 2) % 4, r % 2


def send(src, dst, send_sem, recv_sem, where):
    return pltpu.make_async_remote_copy(
        src_ref=src, dst_ref=dst, send_sem=send_sem, recv_sem=recv_sem, device_id=where, device_id_type=MESH
    )


class Gather:
    def __init__(self, buf, sz, rz, sx, rx, sc, rc):
        self.buf, self.sz, self.rz, self.sx, self.rx, self.sc, self.rc = buf, sz, rz, sx, rx, sc, rc
        _, self.r, _, self.z, self.x, self.core = place()

    def along_z(self, source, d):
        target = (self.z + d) % NZ
        block = self.buf.at[source, self.x, self.core]
        return send(block, block, self.sz.at[d - 1], self.rz.at[source], {"row": target * 8 + self.x * 2 + self.core})

    def along_x(self, source, e):
        target = (self.x + e) % NX
        block = self.buf.at[source, self.x, self.core]
        return send(block, block, self.sx.at[source, e - 1], self.rx.at[source, self.x],
                    {"row": self.z * 8 + target * 2 + self.core})

    def from_x(self, source, e):
        x = (self.x + e) % NX
        block = self.buf.at[source, x, self.core]
        return send(block, block, self.sx.at[source, 0], self.rx.at[source, x], {"row": self.r + 1 - 2 * self.core})

    def across(self, source, core):
        block = self.buf.at[source, :, core]
        return send(block, block, self.sc.at[source], self.rc.at[source], {"row": self.r + 1 - 2 * self.core})

    def run(self):
        z = self.z
        for d in range(1, NZ):
            self.along_z(z, d).start()
        for e in range(1, NX):
            self.along_x(z, e).start()

        def forward(d, carry):
            source = (z + NZ - d) % NZ
            self.along_z(source, 1).wait_recv()
            for e in range(1, NX):
                self.along_x(source, e).start()
            return carry

        lax.fori_loop(1, NZ, forward, 0)

        def swap(d, carry):
            source = (z + NZ - d) % NZ
            for e in range(1, NX):
                self.from_x(source, e).wait_recv()
            self.across(source, self.core).start()
            return carry

        lax.fori_loop(0, NZ, swap, 0)

        def arrive(source, carry):
            self.across(source, 1 - self.core).wait_recv()
            return carry

        lax.fori_loop(0, NZ, arrive, 0)

    def finish(self):
        for d in range(1, NZ):
            self.along_z(self.z, d).wait_send()

        def drain(source, carry):
            for e in range(1, NX):
                self.along_x(source, e).wait_send()
            self.across(source, self.core).wait_send()
            return carry

        lax.fori_loop(0, NZ, drain, 0)


def gather_sems():
    dma = pltpu.SemaphoreType.DMA
    return [dma((NZ - 1,)), dma((NZ,)), dma((NZ, NX - 1)), dma((NZ, NX)), dma((NZ,)), dma((NZ,))]


def greet():
    h, r, c, z, x, core = place()
    barrier = pltpu.get_barrier_semaphore()
    peers = [{"row": (z + d) % NZ * 8 + x * 2 + core} for d in range(1, NZ)]
    peers += [{"row": z * 8 + (x + e) % NX * 2 + core} for e in range(1, NX)]
    peers += [{"row": r + 1 - 2 * core}]
    peers += [{"col": (c + e) % NCOL} for e in range(1, NCOL)]
    peers += [{"gen": 1 - h}]
    for peer in peers:
        pl.semaphore_signal(barrier, inc=1, device_id=peer, device_id_type=MESH)
    pl.semaphore_wait(barrier, len(peers))


def front_kernel(factor, lanes, mine, diag, points, bulk, fv, pan, u, dgat, dy, dg, ybuf, local, sdy, rdy, sdg, rdg, sy, ry, *sems):
    h, r, c, z, x, core = place()
    load = pltpu.make_async_copy(factor, fv, local.at[0])
    rows = pltpu.make_async_copy(factor.at[pl.ds(0, PAN), :], pan.at[z, x, core, :, pl.ds(0, DEPTH)], local.at[1])
    marks = pltpu.make_async_copy(lanes, pan.at[z, x, core, :, pl.ds(DEPTH, 128)], local.at[2])
    rows.start()
    marks.start()
    load.start()
    greet()
    rows.wait()
    marks.wait()
    first = Gather(pan, *sems[:6])
    second = Gather(dgat, *sems[6:])
    first.run()
    load.wait()

    def y_small(e):
        return send(u.at[pl.ds(0, PAN), :], dy.at[e - 1], sdy.at[e - 1], rdy.at[e - 1], {"col": (c + e) % NCOL})

    def y_large(e):
        part = (c + e) % NCOL
        return send(u.at[pl.ds(part * QUART, QUART), :], ybuf.at[e - 1], sy.at[e - 1], ry.at[e - 1], {"col": part})

    gen_small = send(dy.at[NCOL - 1], dg, sdg.at[0], rdg.at[0], {"gen": 1 - h})

    def multiply(q, carry):
        at = pl.ds(pl.multiple_of(q * QUART, QUART), QUART)
        panel = pan[:, :, :, :, :DEPTH].reshape(B, DEPTH)
        u[at, :] = dotf(fv[at, :], panel, ((1,), (1,)))

        @pl.when(q == 0)
        def _():
            for e in range(1, NCOL):
                y_small(e).start()

        return carry

    lax.fori_loop(0, NCOL, multiply, 0)
    for e in range(1, NCOL):
        y_small(e).wait_recv()
    dy[NCOL - 1] = u[:PAN, :] + dy[0] + dy[1] + dy[2]
    gen_small.start()
    for e in range(1, NCOL):
        y_large(e).start()
    marks8 = pan[:, :, :, :, DEPTH:].reshape(4, 16, PAN, 128)
    for q in range(4):
        total = marks8[q, 0]
        for i in range(1, 16):
            total = total + marks8[q, i]
        points[:, 128 * q : 128 * q + 128] = total
    px = jnp.broadcast_to(mine[:, :1], (PAN, B))
    py = jnp.broadcast_to(mine[:, 128:129], (PAN, B))
    sub = lax.broadcasted_iota(jnp.int32, (PAN, B), 0)
    lane = lax.broadcasted_iota(jnp.int32, (PAN, B), 1)
    same = jnp.where(lane == sub + PAN * r, jnp.float32(nugget_term), jnp.float32(0))
    kern = matern(px - points[0:1, :], py - points[1:2, :]) + same
    gen_small.wait_recv()
    dgat[z, x, core] = kern - (dy[NCOL - 1] + dg[...])
    second.run()
    diag[...] = dgat[...].reshape(B, B)
    for e in range(1, NCOL):
        y_large(e).wait_recv()
    here = pl.ds(pl.multiple_of(c * QUART, QUART), QUART)
    bulk[...] = u[here, :] + ybuf[0] + ybuf[1] + ybuf[2]
    for e in range(1, NCOL):
        y_small(e).wait_send()
        y_large(e).wait_send()
    gen_small.wait_send()
    first.finish()
    second.finish()


def front(factor, lanes, mine):
    dma = pltpu.SemaphoreType.DMA
    f32 = jnp.float32
    vmem = pl.BlockSpec(memory_space=pltpu.VMEM)
    return pl.pallas_call(
        front_kernel,
        out_shape=[
            jax.ShapeDtypeStruct((B, B), f32),
            jax.ShapeDtypeStruct((PAN, B), f32),
            jax.ShapeDtypeStruct((QUART, B), f32),
        ],
        in_specs=[pl.BlockSpec(memory_space=pl.ANY), vmem, vmem],
        out_specs=[vmem, vmem, vmem],
        scratch_shapes=[
            pltpu.VMEM((ROWS, DEPTH), f32),
            pltpu.VMEM((NZ, NX, NC, PAN, WIDE), f32),
            pltpu.VMEM((ROWS, B), f32),
            pltpu.VMEM((NZ, NX, NC, PAN, B), f32),
            pltpu.VMEM((NCOL, PAN, B), f32),
            pltpu.VMEM((PAN, B), f32),
            pltpu.VMEM((NCOL - 1, QUART, B), f32),
            dma((3,)), dma((3,)), dma((3,)), dma((1,)), dma((1,)), dma((3,)), dma((3,)),
            *gather_sems(), *gather_sems(),
        ],
        compiler_params=pltpu.CompilerParams(
            collective_id=0, has_side_effects=True, vmem_limit_bytes=48 << 20
        ),
        name="front",
    )(factor, lanes, mine)


def chol_kernel(d_ref, out_ref, work, tile, inv):
    n = 4
    work[...] = d_ref[...]
    out_ref[...] = jnp.zeros((B, B), jnp.float32)

    def step(k, carry):
        for v in range(n):
            @pl.when(k == v)
            def _():
                tile[...] = work[128 * v : 128 * v + 128, 128 * v : 128 * v + 128]
        inverse_factor(tile, inv)
        for v in range(n):
            @pl.when(k == v)
            def _():
                lo, hi = 128 * v, 128 * v + 128
                t = inv[...]
                if v:
                    out_ref[lo:hi, :lo] = dotf(t, out_ref[lo:hi, :lo], ((1,), (0,)))
                out_ref[lo:hi, lo:hi] = t
                if v < n - 1:
                    r = dotf(t, work[lo:hi, hi:], ((1,), (0,)))
                    work[hi:, hi:] = work[hi:, hi:] - dotf(r, r, ((0,), (0,)))
                    out_ref[hi:, :hi] = out_ref[hi:, :hi] - dotf(r, out_ref[lo:hi, :hi], ((0,), (0,)))
        return carry

    lax.fori_loop(0, n, step, 0)


def inverse_lower(d):
    vmem = pl.BlockSpec(memory_space=pltpu.VMEM)
    return pl.pallas_call(
        chol_kernel,
        out_shape=jax.ShapeDtypeStruct((B, B), jnp.float32),
        in_specs=[vmem],
        out_specs=vmem,
        scratch_shapes=[
            pltpu.VMEM((B, B), jnp.float32),
            pltpu.VMEM((128, 128), jnp.float32),
            pltpu.VMEM((128, 128), jnp.float32),
        ],
        compiler_params=pltpu.CompilerParams(vmem_limit_bytes=16 << 20),
        cost_estimate=pl.CostEstimate(flops=200_000_000_000, bytes_accessed=2 << 20, transcendentals=0),
        name="inverse_lower",
    )(d)


def shards(coords, factor):
    h, r, c = lax.axis_index("gen"), lax.axis_index("row"), lax.axis_index("col")
    points = coords.astype(jnp.float32) / GRID
    lane = lax.broadcasted_iota(jnp.int32, (PAN, 128), 1)
    sub = lax.broadcasted_iota(jnp.int32, (PAN, 128), 0)
    lanes = jnp.zeros((PAN, 128), jnp.float32)
    for j in range(PAN):
        value = jnp.where(sub == 0, points[0, j], jnp.where(sub == 1, points[1, j], 0.0))
        lanes = jnp.where(lane == (r % 16) * PAN + j, value, lanes)
    mine = jnp.broadcast_to(points[:, :PAN].T[:, :, None], (PAN, 2, 128)).reshape(PAN, 256)
    diag, pan_points, bulk = front(factor, lanes, mine)
    other = lax.ppermute(bulk, "gen", [(0, 1), (1, 0)])
    inverse = inverse_lower(diag)
    here = lax.dynamic_slice_in_dim(points, c * QUART, QUART, 1)
    ids = c * QUART + jnp.arange(QUART, dtype=jnp.int32)
    columns = jnp.arange(B, dtype=jnp.int32)
    same = (ids[:, None] < PAN) & (columns[None, :] == r * PAN + ids[:, None])
    kern = matern(here[0][:, None] - pan_points[0][None, :], here[1][:, None] - pan_points[1][None, :])
    kern = kern + jnp.where(same, jnp.float32(nugget_term), jnp.float32(0.0))
    updated = kern - (bulk + other)
    wanted = lax.dynamic_slice_in_dim(inverse, h * 256, 256, 0)
    solved = dotf(updated, wanted, ((1,), (1,)))
    blocks = []
    for e in range(NCOL):
        part = lax.dynamic_slice_in_dim(solved, (c + e) % NCOL * 64, 64, 1)
        blocks.append(lax.ppermute(part, "col", [(i, (i + e) % NCOL) for i in range(NCOL)]) if e else part)
    out = jnp.zeros((ROWS, 64), jnp.float32)
    for e in range(NCOL):
        out = lax.dynamic_update_slice_in_dim(out, blocks[e], (c + NCOL - e) % NCOL * QUART, 0)
    return out


def solution(mesh):
    in_specs = (P(None, "row"), P("row", ("gen", "col")))
    out_specs = P("row", ("gen", "col"))
    return jax.shard_map(shards, mesh=mesh, in_specs=in_specs, out_specs=out_specs, check_vma=False)
```

time: 670 us -> 158 us (0.24)
  the two profiles are of different devices: /device:TPU:1 before, /device:TPU:168 now
where the time goes in v1:
time: 158 us
  Pallas kernels  87.2 us (55%)
  waiting for transfers between devices  37.9 us (24%)
  starting transfers between devices  14.5 us (9%)
  other arithmetic  10.9 us (7%)
  local copies, waits for them, and re-layouts  4.53 us (3%)
  matrix products  2.33 us (1%)
    pallas_call x1, Pallas kernels, front(): pl.pallas_call(front_kernel, out_shape=[jax.ShapeDtypeStruct((B, B), f32)...  67.7 us
    ppermute x1, waiting for transfers between devices, shards(): other = lax.ppermute(bulk, 'gen', [(0, 1), (1, 0)])  33.7 us
    pallas_call x1, Pallas kernels, inverse_lower(): pl.pallas_call(chol_kernel, out_shape=jax.ShapeDtypeStruct((B, B), jnp.fl...  19.5 us
    ppermute x3, starting transfers between devices, shards(): lax.ppermute(part, 'col', [(i, (i + e) % NCOL) for i in range(NCOL)])  9.86 us
    select_n x1, other arithmetic, shards(): lanes = jnp.where(lane == r % 16 * PAN + j, value, lanes)  5.33 us
    select_n x4, other arithmetic, shards(): jnp.where(sub == 1, points[1, j], 0.0)  4.86 us
    ppermute x1, starting transfers between devices, shards(): other = lax.ppermute(bulk, 'gen', [(0, 1), (1, 0)])  4.63 us
    ppermute x3, waiting for transfers between devices, shards(): lax.ppermute(part, 'col', [(i, (i + e) % NCOL) for i in range(NCOL)])  4.18 us
  transfers between devices with their start and end apart: 4, of which 3 were waited for; matrix products, arithmetic and copies ran while one was open for 1% of the time, Pallas kernels for 12%

profile of v1, /device:TPU:168, one launch (start us, length us, event | category | flops | bytes accessed | tf_op | source)
XLA Modules:
  0.0 157.7 jit_solution(4509369745400202346)
XLA Ops:
  0.0 0.7 convert_multiply_fusion
  0.7 0.0 copy-start.2
  0.7 0.7 fusion.43
  1.4 0.0 copy-done.2
  1.5 0.1 broadcast_bitcast_fusion.mine
  1.6 1.2 fusion.37
  2.8 1.3 fusion.35
  4.1 1.2 fusion.33
  5.3 1.2 fusion.31
  6.5 5.3 %select_select_fusion.lanes = f32[8,128]{1,0:T(8,128)S(1)} fusion(f32[8]{0:T(128)S(1)} %get-tuple-element.43, f32[]{:T(128)} %bitcast.15, f32[8]{0:T(128)S(1)} %get-tuple-element.44, f32[]{:T(128)} %bitcast.13, f32[8]{0:T(128)S(1)} %get-tuple-element.45, f32[]{:T(128)} %bitcast.11, f32[8]{0:T(128)S(1)} %get-tuple-element.46, f32[]{:T(128)} %bitcast.9, ...), kind=kLoop, calls=%fused_computation.31 | loop fusion | flops 16384 | bytes 5416 | tf_op jit(solution)/shard_map/jit(_where)/select_n | solution.py:331
  11.8 0.0 copy-start
  11.8 2.2 %copy-done = f32[1024,1024]{1,0:T(8,128)S(1)} copy-done((f32[1024,1024]{1,0:T(8,128)S(1)}, f32[1024,1024]{1,0:T(8,128)}, u32[]{:S(2)}) %copy-start) | copy-done | bytes 4194328
  14.0 67.7 %front.1 = (f32[512,512]{1,0:T(8,128)S(1)}, f32[8,512]{1,0:T(8,128)S(1)}, f32[256,512]{1,0:T(8,128)}) custom-call(f32[1024,1024]{1,0:T(8,128)S(1)} %copy-done, f32[8,128]{1,0:T(8,128)S(1)} %select_select_fusion.lanes, f32[8,256]{1,0:T(8,128)S(1)} %broadcast_bitcast_fusion.mine), custom_call_target="tpu_custom_call" | custom-call | tf_op jit(solution)/shard_map/front/pallas_call | solution.py:250
  81.7 4.6 %collective-permute-start = (f32[256,512]{1,0:T(8,128)}, f32[256,512]{1,0:T(8,128)}, u32[]{:S(2)}, u32[]{:S(2)}) collective-permute-start(f32[256,512]{1,0:T(8,128)} %get-tuple-element.9), channel_id=1, source_target_pairs={{0,256},{256,0},{1,257},{257,1},{2,258},{258,2},{3,259},{259,3},{4... | collective-permute-start | bytes 1572872 | tf_op jit(solution)/shard_map/ppermute | solution.py:334
  86.4 19.5 %inverse_lower.1 = f32[512,512]{1,0:T(8,128)S(1)} custom-call(f32[512,512]{1,0:T(8,128)S(1)} %get-tuple-element.10.d_ref), custom_call_target="tpu_custom_call" | custom-call | flops 199999995904 | bytes 2097152 | tf_op jit(solution)/shard_map/inverse_lower/pallas_call | solution.py:307
  105.9 0.8 constant_dynamic-slice_fusion.3
  106.8 33.7 %collective-permute-done = f32[256,512]{1,0:T(8,128)} collective-permute-done((f32[256,512]{1,0:T(8,128)}, f32[256,512]{1,0:T(8,128)}, u32[]{:S(2)}, u32[]{:S(2)}) %collective-permute-start) | collective-permute-done | bytes 524320 | tf_op jit(solution)/shard_map/ppermute | solution.py:334
  140.5 2.3 %fusion = f32[256,256]{0,1:T(8,128)S(1)} fusion(f32[512,512]{1,0:T(8,128)S(1)} %inverse_lower.1, s32[]{:T(128)S(6)} %select_n.191, f32[256,512]{1,0:T(8,128)} %get-tuple-element.9, f32[256,512]{1,0:T(8,128)} %collective-permute-done, s32[256]{0:T(256)S(1)} %fusion.29, f32[512]{0:T(512)S(1)} %bitcast.25, f32[256]{0:T(256)S(1)} %bitcast.27, ...), kind=kOutput, calls=%fused_computation | convolution fusion | flops 404619264 | bytes 1842692 | tf_op jit(solution)/shard_map/dot_general | solution.py:26
  142.9 3.4 %collective-permute-start.1 = (f32[256,64]{0,1:T(8,128)S(1)}, f32[256,64]{0,1:T(8,128)S(1)}, u32[]{:S(2)}, u32[]{:S(2)}) collective-permute-start(f32[256,64]{0,1:T(8,128)S(1)} %get-tuple-element.13), channel_id=1, source_target_pairs={{0,1},{1,2},{2,3},{3,0},{4,5},{5,6},{6,7},{7,4},{8,9},{9,10},{10,1... | collective-permute-start | bytes 196616 | tf_op jit(solution)/shard_map/ppermute | solution.py:348
  146.3 4.6 %collective-permute-start.2 = (f32[256,64]{0,1:T(8,128)S(1)}, f32[256,64]{0,1:T(8,128)S(1)}, u32[]{:S(2)}, u32[]{:S(2)}) collective-permute-start(f32[256,64]{0,1:T(8,128)S(1)} %get-tuple-element.12), channel_id=1, source_target_pairs={{0,2},{1,3},{2,0},{3,1},{4,6},{5,7},{6,4},{7,5},{8,10},{9,11},{10,... | collective-permute-start | bytes 196616 | tf_op jit(solution)/shard_map/ppermute | solution.py:348
  150.9 1.9 %collective-permute-start.3 = (f32[256,64]{0,1:T(8,128)S(1)}, f32[256,64]{0,1:T(8,128)S(1)}, u32[]{:S(2)}, u32[]{:S(2)}) collective-permute-start(f32[256,64]{0,1:T(8,128)S(1)} %get-tuple-element.11), channel_id=1, source_target_pairs={{0,3},{1,0},{2,1},{3,2},{4,7},{5,4},{6,5},{7,6},{8,11},{9,8},{10,9... | collective-permute-start | bytes 196616 | tf_op jit(solution)/shard_map/ppermute | solution.py:348
  152.8 0.0 collective-permute-done.1
  152.8 1.2 collective-permute-done.2
  154.1 0.0 copy-start.1
  154.1 3.0 %collective-permute-done.3 = f32[256,64]{0,1:T(8,128)S(1)} collective-permute-done((f32[256,64]{0,1:T(8,128)S(1)}, f32[256,64]{0,1:T(8,128)S(1)}, u32[]{:S(2)}, u32[]{:S(2)}) %collective-permute-start.3) | collective-permute-done | bytes 65568 | tf_op jit(solution)/shard_map/ppermute | solution.py:348
  157.0 0.0 copy-done.1
  157.1 0.6 constant_dynamic-update-slice_fusion
  (13 shorter events, 0.1 us)
Async XLA Ops:
  0.7 0.7 copy-start.2
  11.8 2.2 %copy-start = (f32[1024,1024]{1,0:T(8,128)S(1)}, f32[1024,1024]{1,0:T(8,128)}, u32[]{:S(2)}) copy-start(f32[1024,1024]{1,0:T(8,128)} %factor.1) | copy-start | bytes 12582916
  81.7 58.8 %collective-permute-start = (f32[256,512]{1,0:T(8,128)}, f32[256,512]{1,0:T(8,128)}, u32[]{:S(2)}, u32[]{:S(2)}) collective-permute-start(f32[256,512]{1,0:T(8,128)} %get-tuple-element.9), channel_id=1, source_target_pairs={{0,256},{256,0},{1,257},{257,1},{2,258},{258,2},{3,259},{259,3},{4... | collective-permute-start | bytes 1572872 | tf_op jit(solution)/shard_map/ppermute | solution.py:334
  142.9 9.9 %collective-permute-start.1 = (f32[256,64]{0,1:T(8,128)S(1)}, f32[256,64]{0,1:T(8,128)S(1)}, u32[]{:S(2)}, u32[]{:S(2)}) collective-permute-start(f32[256,64]{0,1:T(8,128)S(1)} %get-tuple-element.13), channel_id=1, source_target_pairs={{0,1},{1,2},{2,3},{3,0},{4,5},{5,6},{6,7},{7,4},{8,9},{9,10},{10,1... | collective-permute-start | bytes 196616 | tf_op jit(solution)/shard_map/ppermute | solution.py:348
  146.3 7.7 %collective-permute-start.2 = (f32[256,64]{0,1:T(8,128)S(1)}, f32[256,64]{0,1:T(8,128)S(1)}, u32[]{:S(2)}, u32[]{:S(2)}) collective-permute-start(f32[256,64]{0,1:T(8,128)S(1)} %get-tuple-element.12), channel_id=1, source_target_pairs={{0,2},{1,3},{2,0},{3,1},{4,6},{5,7},{6,4},{7,5},{8,10},{9,11},{10,... | collective-permute-start | bytes 196616 | tf_op jit(solution)/shard_map/ppermute | solution.py:348
  150.9 6.2 %collective-permute-start.3 = (f32[256,64]{0,1:T(8,128)S(1)}, f32[256,64]{0,1:T(8,128)S(1)}, u32[]{:S(2)}, u32[]{:S(2)}) collective-permute-start(f32[256,64]{0,1:T(8,128)S(1)} %get-tuple-element.11), channel_id=1, source_target_pairs={{0,3},{1,0},{2,1},{3,2},{4,7},{5,4},{6,5},{7,6},{8,11},{9,8},{10,9... | collective-permute-start | bytes 196616 | tf_op jit(solution)/shard_map/ppermute | solution.py:348
  154.1 3.0 %copy-start.1 = (f32[1024,64]{0,1:T(8,128)}, f32[1024,64]{0,1:T(8,128)S(1)}, u32[]{:S(2)}) copy-start(f32[1024,64]{0,1:T(8,128)S(1)} %constant_dynamic-update-slice_fusion.1) | copy-start | bytes 786436

commit v2 on v1

v2 whole, which is shorter than its diff:
```python
import jax
import jax.numpy as jnp
from jax import lax
from jax.experimental import pallas as pl
from jax.experimental.pallas import tpu as pltpu
from jax.sharding import PartitionSpec as P

B = 512
GRID = 1024
PAN = 8
ROWS = 1024
DEPTH = 1024
HALF = 128
NZ, NX, NC, NCOL = 8, 4, 2, 4
WIDE = DEPTH + 128

root_three = 1.7320508075688772
length_scale = 0.2
nugget_term = 1.0

HI = lax.Precision.HIGHEST
MESH = pl.DeviceIdType.MESH


def dotf(a, b, dims):
    return lax.dot_general(a, b, (dims, ((), ())), precision=HI, preferred_element_type=jnp.float32)


def matern(delta_x, delta_y):
    scaled = root_three * jnp.sqrt(delta_x * delta_x + delta_y * delta_y) / length_scale
    return (1.0 + scaled) * jnp.exp(-scaled)


def spread(x, k):
    return jnp.broadcast_to(x[k : k + 1], x.shape)


def inverse_factor(tile_ref, out_ref):
    sub = lax.broadcasted_iota(jnp.int32, (8, 128), 0)
    lane = lax.broadcasted_iota(jnp.int32, (8, 128), 1)
    a = [tile_ref[8 * i : 8 * i + 8, :] for i in range(16)]
    t = [jnp.where(lane == sub + 8 * i, jnp.float32(1), jnp.float32(0)) for i in range(16)]
    for b in range(16):
        cols = [jnp.broadcast_to(a[b][:, 8 * b + k : 8 * b + k + 1], (8, 128)) for k in range(8)]
        recip, cross, scale = [], [], jnp.ones((8, 128), jnp.float32)
        for k in range(8):
            pivot = spread(cols[k], k)
            r = 1.0 / pivot
            recip.append(r)
            scale = jnp.where(sub == k, pivot, scale)
            m = jnp.where(sub > k, cols[k] * r, 0.0)
            row = []
            for j in range(k + 1, 8):
                s = spread(cols[j], k)
                row.append(s)
                cols[j] = cols[j] - m * s
            cross.append(row)
            a[b] = a[b] - m * spread(a[b], k)
            t[b] = t[b] - m * spread(t[b], k)
        ua = [spread(a[b], k) for k in range(8)]
        ut = [spread(t[b], k) for k in range(8)]
        out_ref[8 * b : 8 * b + 8, :] = t[b] * lax.rsqrt(scale)
        for i in range(b + 1, 16):
            c = [jnp.broadcast_to(a[i][:, 8 * b + k : 8 * b + k + 1], (8, 128)) for k in range(8)]
            da = dt = None
            for k in range(8):
                m = c[k] * recip[k]
                for j in range(k + 1, 8):
                    c[j] = c[j] - m * cross[k][j - k - 1]
                da = m * ua[k] if da is None else da + m * ua[k]
                dt = m * ut[k] if dt is None else dt + m * ut[k]
            a[i] = a[i] - da
            t[i] = t[i] - dt


def place():
    h, r, c = lax.axis_index("gen"), lax.axis_index("row"), lax.axis_index("col")
    return h, r, c, r // 8, (r // 2) % 4, r % 2


def send(src, dst, send_sem, recv_sem, where):
    return pltpu.make_async_remote_copy(
        src_ref=src, dst_ref=dst, send_sem=send_sem, recv_sem=recv_sem, device_id=where, device_id_type=MESH
    )


class Gather:
    def __init__(self, buf, sz, rz, sx, rx, sc, rc):
        self.buf, self.sz, self.rz, self.sx, self.rx, self.sc, self.rc = buf, sz, rz, sx, rx, sc, rc
        _, self.r, _, self.z, self.x, self.core = place()

    def along_z(self, source, d):
        target = (self.z + d) % NZ
        block = self.buf.at[source, self.x, self.core]
        return send(block, block, self.sz.at[d - 1], self.rz.at[source], {"row": target * 8 + self.x * 2 + self.core})

    def along_x(self, source, e):
        target = (self.x + e) % NX
        block = self.buf.at[source, self.x, self.core]
        return send(block, block, self.sx.at[source, e - 1], self.rx.at[source, self.x],
                    {"row": self.z * 8 + target * 2 + self.core})

    def from_x(self, source, e):
        x = (self.x + e) % NX
        block = self.buf.at[source, x, self.core]
        return send(block, block, self.sx.at[source, 0], self.rx.at[source, x], {"row": self.r + 1 - 2 * self.core})

    def across(self, source, core):
        block = self.buf.at[source, :, core]
        return send(block, block, self.sc.at[source], self.rc.at[source], {"row": self.r + 1 - 2 * self.core})

    def run(self):
        z = self.z
        for d in range(1, NZ):
            self.along_z(z, d).start()
        for e in range(1, NX):
            self.along_x(z, e).start()

        def forward(d, carry):
            source = (z + NZ - d) % NZ
            self.along_z(source, 1).wait_recv()
            for e in range(1, NX):
                self.along_x(source, e).start()
            return carry

        lax.fori_loop(1, NZ, forward, 0)

        def swap(d, carry):
            source = (z + NZ - d) % NZ
            for e in range(1, NX):
                self.from_x(source, e).wait_recv()
            self.across(source, self.core).start()
            return carry

        lax.fori_loop(0, NZ, swap, 0)

        def arrive(source, carry):
            self.across(source, 1 - self.core).wait_recv()
            return carry

        lax.fori_loop(0, NZ, arrive, 0)

    def finish(self):
        for d in range(1, NZ):
            self.along_z(self.z, d).wait_send()

        def drain(source, carry):
            for e in range(1, NX):
                self.along_x(source, e).wait_send()
            self.across(source, self.core).wait_send()
            return carry

        lax.fori_loop(0, NZ, drain, 0)


def gather_sems():
    dma = pltpu.SemaphoreType.DMA
    return [dma((NZ - 1,)), dma((NZ,)), dma((NZ, NX - 1)), dma((NZ, NX)), dma((NZ,)), dma((NZ,))]


def greet():
    h, r, c, z, x, core = place()
    barrier = pltpu.get_barrier_semaphore()
    peers = [{"row": (z + d) % NZ * 8 + x * 2 + core} for d in range(1, NZ)]
    peers += [{"row": z * 8 + (x + e) % NX * 2 + core} for e in range(1, NX)]
    peers += [{"row": r + 1 - 2 * core}]
    peers += [{"col": (c + e) % NCOL} for e in range(1, NCOL)]
    peers += [{"gen": 1 - h, "col": (c + e) % NCOL} for e in range(NCOL)]
    for peer in peers:
        pl.semaphore_signal(barrier, inc=1, device_id=peer, device_id_type=MESH)
    pl.semaphore_wait(barrier, len(peers))


def halves(x):
    high = x.astype(jnp.bfloat16)
    return high, (x - high.astype(jnp.float32)).astype(jnp.bfloat16)


def three(a, b):
    dims = (((1,), (1,)), ((), ()))
    f32 = jnp.float32
    total = lax.dot_general(a[0], b[1], dims, preferred_element_type=f32)
    total += lax.dot_general(a[1], b[0], dims, preferred_element_type=f32)
    return total + lax.dot_general(a[0], b[0], dims, preferred_element_type=f32)


def step_kernel(
    coords, factor, out, fv, pan, high, low, u, dgat, dy, dg, ybuf, gout, gbuf, marks, points, upd,
    work, tile, inv, linv, xs, xt, local, sdy, rdy, sdg, rdg, sy, ry, sg, rg, sx, rx, *sems,
):
    h, r, c, z, x, core = place()
    f32 = jnp.float32
    load = pltpu.make_async_copy(factor, fv, local.at[0])
    rows = pltpu.make_async_copy(factor.at[0, 0, pl.ds(0, PAN), :], pan.at[z, x, core, :, pl.ds(0, DEPTH)], local.at[1])
    rows.start()
    load.start()

    sub = lax.broadcasted_iota(jnp.int32, (PAN, 128), 0)
    lane = lax.broadcasted_iota(jnp.int32, (PAN, 128), 1)
    start = coords[:, :128].astype(f32) / GRID
    mark = jnp.zeros((PAN, 128), f32)
    own_x, own_y = mark, mark
    for j in range(PAN):
        px = jnp.broadcast_to(start[0:1, j : j + 1], (PAN, 128))
        py = jnp.broadcast_to(start[1:2, j : j + 1], (PAN, 128))
        own_x = jnp.where(sub == j, px, own_x)
        own_y = jnp.where(sub == j, py, own_y)
        both = jnp.where(sub == 0, px, jnp.where(sub == 1, py, 0.0))
        mark = jnp.where(lane == (r % 16) * PAN + j, both, mark)
    marks[...] = mark
    tag = pltpu.make_async_copy(marks, pan.at[z, x, core, :, pl.ds(DEPTH, 128)], local.at[2])
    tag.start()
    greet()
    rows.wait()
    tag.wait()
    first = Gather(pan, *sems[:6])
    second = Gather(dgat, *sems[6:])
    first.run()
    load.wait()

    def y_small(e):
        return send(u.at[0, 0, pl.ds(0, PAN), :], dy.at[e - 1], sdy.at[e - 1], rdy.at[e - 1], {"col": (c + e) % NCOL})

    def y_large(s, e):
        part = (c + e) % NCOL
        return send(u.at[part, s], ybuf.at[s, e - 1], sy.at[s, e - 1], ry.at[s, e - 1], {"col": part})

    gen_small = send(dy.at[NCOL - 1], dg, sdg.at[0], rdg.at[0], {"gen": 1 - h})
    gen_large = send(gout, gbuf, sg.at[0], rg.at[0], {"gen": 1 - h})

    high[...], low[...] = halves(pan[:, :, :, :, :DEPTH].reshape(B, DEPTH))

    def multiply(s):
        a = halves(fv[:, s].reshape(4 * HALF, DEPTH))
        u[:, s] = three(a, (high[...], low[...])).reshape(4, HALF, B)

    multiply(0)
    for e in range(1, NCOL):
        y_small(e).start()

    @pl.when(h == 1)
    def _():
        for e in range(1, NCOL):
            y_large(0, e).start()

    multiply(1)

    for e in range(1, NCOL):
        y_small(e).wait_recv()
    dy[NCOL - 1] = u[0, 0, :PAN, :] + dy[0] + dy[1] + dy[2]
    gen_small.start()

    @pl.when(h == 0)
    def _():
        for e in range(1, NCOL):
            y_large(1, e).start()

    for e in range(1, NCOL):
        y_large(h, e).start()

    grouped = pan[:, :, :, :, DEPTH:].reshape(4, 16, PAN, 128)
    for q in range(4):
        total = grouped[q, 0]
        for i in range(1, 16):
            total = total + grouped[q, i]
        points[:, 128 * q : 128 * q + 128] = total
    kern = []
    for q in range(4):
        at = slice(128 * q, 128 * q + 128)
        same = jnp.where(lane + 128 * q == sub + PAN * r, f32(nugget_term), f32(0))
        kern.append(matern(own_x - points[0:1, at], own_y - points[1:2, at]) + same)
    gen_small.wait_recv()
    for q in range(4):
        at = slice(128 * q, 128 * q + 128)
        dgat[z, x, core, :, at] = kern[q] - (dy[NCOL - 1, :, at] + dg[:, at])
    second.run()
    work[...] = dgat[...].reshape(B, B)

    for e in range(1, NCOL):
        y_large(1 - h, e).wait_recv()
    gout[...] = u[c, 1 - h] + ybuf[1 - h, 0] + ybuf[1 - h, 1] + ybuf[1 - h, 2]
    gen_large.start()

    linv[...] = jnp.zeros((B, B), f32)

    def combine():
        for e in range(1, NCOL):
            y_large(h, e).wait_recv()
        here = pl.ds(pl.multiple_of((c * 2 + h) * HALF, HALF), HALF)
        mx = jnp.broadcast_to(coords[0:1, here].astype(f32) / GRID, (HALF, HALF)).T
        my = jnp.broadcast_to(coords[1:2, here].astype(f32) / GRID, (HALF, HALF)).T
        isub = lax.broadcasted_iota(jnp.int32, (HALF, 128), 0) + (c * 2 + h) * HALF
        ilane = lax.broadcasted_iota(jnp.int32, (HALF, 128), 1)
        for q in range(4):
            at = slice(128 * q, 128 * q + 128)
            same = (isub < PAN) & (ilane + 128 * q == isub + PAN * r)
            k = matern(mx - points[0:1, at], my - points[1:2, at]) + jnp.where(same, f32(nugget_term), f32(0))
            part = u[c, h, :, at] + ybuf[h, 0, :, at] + ybuf[h, 1, :, at] + ybuf[h, 2, :, at]
            upd[:, at] = k - part

    def settle():
        gen_large.wait_recv()
        upd[...] = upd[...] - gbuf[...]

    slot = c * 2 + h

    def deliver(g):
        return send(
            xs.at[g], xt.at[slot], sx.at[g], rx.at[slot], {"gen": g // NCOL, "col": g % NCOL}
        )

    def solve(v):
        lo, hi = 128 * v, 128 * v + 128
        block = dotf(linv[lo:hi, :hi], upd[:, :hi], ((1,), (1,)))
        for i in range(2):
            g = 2 * v + i
            xs[g] = block[64 * i : 64 * i + 64]

            @pl.when(h * NCOL + c == g)
            def _():
                xt[slot] = xs[g]

            @pl.when(h * NCOL + c != g)
            def _():
                deliver(g).start()

    def step(k, carry):
        for v in range(4):
            @pl.when(k == v)
            def _():
                tile[...] = work[128 * v : 128 * v + 128, 128 * v : 128 * v + 128]
        inverse_factor(tile, inv)
        for v in range(4):
            @pl.when(k == v)
            def _():
                lo, hi = 128 * v, 128 * v + 128
                t = inv[...]
                if v:
                    linv[lo:hi, :lo] = dotf(t, linv[lo:hi, :lo], ((1,), (0,)))
                linv[lo:hi, lo:hi] = t
                if v < 3:
                    p = dotf(t, work[lo:hi, hi:], ((1,), (0,)))
                    work[hi:, hi:] = work[hi:, hi:] - dotf(p, p, ((0,), (0,)))
                    linv[hi:, :hi] = linv[hi:, :hi] - dotf(p, linv[lo:hi, :hi], ((0,), (0,)))
                if v == 1:
                    combine()
                if v == 2:
                    settle()
                    for w in range(3):
                        solve(w)
                if v == 3:
                    solve(3)
        return carry

    lax.fori_loop(0, 4, step, 0)

    for g in range(2 * NCOL):
        @pl.when(h * NCOL + c != g)
        def _():
            theirs = (g % NCOL) * 2 + g // NCOL
            send(xs.at[g], xt.at[theirs], sx.at[g], rx.at[theirs], {"gen": g // NCOL, "col": g % NCOL}).wait_recv()

    for i in range(2 * NCOL):
        out[:, HALF * i : HALF * i + HALF] = xt[i]

    for g in range(2 * NCOL):
        @pl.when(h * NCOL + c != g)
        def _():
            deliver(g).wait_send()
    for e in range(1, NCOL):
        y_small(e).wait_send()
        for s in range(2):
            y_large(s, e).wait_send()
    gen_small.wait_send()
    gen_large.wait_send()
    first.finish()
    second.finish()


def shards(coords, factor):
    dma = pltpu.SemaphoreType.DMA
    vmem = pl.BlockSpec(memory_space=pltpu.VMEM)

    def room(*shape, dtype=jnp.float32):
        return pltpu.VMEM(shape, dtype)

    solved = pl.pallas_call(
        step_kernel,
        out_shape=jax.ShapeDtypeStruct((B // 8, ROWS), jnp.float32),
        in_specs=[vmem, pl.BlockSpec(memory_space=pl.ANY)],
        out_specs=vmem,
        scratch_shapes=[
            room(4, 2, HALF, DEPTH),
            room(NZ, NX, NC, PAN, WIDE),
            room(B, DEPTH, dtype=jnp.bfloat16),
            room(B, DEPTH, dtype=jnp.bfloat16),
            room(4, 2, HALF, B),
            room(NZ, NX, NC, PAN, B),
            room(NCOL, PAN, B),
            room(PAN, B),
            room(2, NCOL - 1, HALF, B),
            room(HALF, B),
            room(HALF, B),
            room(PAN, 128),
            room(PAN, B),
            room(HALF, B),
            room(B, B),
            room(128, 128),
            room(128, 128),
            room(B, B),
            room(2 * NCOL, B // 8, HALF),
            room(2 * NCOL, B // 8, HALF),
            dma((3,)), dma((3,)), dma((3,)), dma((1,)), dma((1,)), dma((2, 3)), dma((2, 3)),
            dma((1,)), dma((1,)), dma((8,)), dma((8,)),
            *gather_sems(), *gather_sems(),
        ],
        compiler_params=pltpu.CompilerParams(
            collective_id=0, has_side_effects=True, vmem_limit_bytes=48 << 20
        ),
        name="panel_step",
    )(coords, factor.reshape(4, 2, HALF, DEPTH))
    return solved.T


def solution(mesh):
    in_specs = (P(None, "row"), P("row", ("gen", "col")))
    out_specs = P("row", ("gen", "col"))
    return jax.shard_map(shards, mesh=mesh, in_specs=in_specs, out_specs=out_specs, check_vma=False)
```

time: 158 us -> 115 us (0.73)
  the two profiles are of different devices: /device:TPU:168 before, /device:TPU:1 now
where the time goes in v2:
time: 115 us; the launch traced here: 113 us
  Pallas kernels  110 us (96%)
  local copies, waits for them, and re-layouts  3.59 us (3%)
    pallas_call x1, Pallas kernels, shards(): pl.pallas_call(step_kernel, out_shape=jax.ShapeDtypeStruct((B // 8, ROWS)...  110 us
    unnamed x5, local copies, waits for them, and re-layouts  3.59 us

profile of v2, /device:TPU:1, one launch (start us, length us, event | category | flops | bytes accessed | tf_op | source)
XLA Modules:
  0.0 113.3 jit_solution(10099512791974758237)
XLA Ops:
  0.0 0.0 copy-start
  0.0 2.2 %copy-done = f32[1024,1024]{1,0:T(8,128)S(1)} copy-done((f32[1024,1024]{1,0:T(8,128)S(1)}, f32[1024,1024]{1,0:T(8,128)}, u32[]{:S(2)}) %copy-start) | copy-done | bytes 4194328
  2.2 0.0 copy-start.1
  2.2 0.7 copy-done.1
  2.9 109.7 %panel_step.1 = f32[64,1024]{1,0:T(8,128)S(1)} custom-call(s32[2,1024]{1,0:T(2,128)S(1)} %copy-done.1, f32[4,2,128,1024]{3,2,1,0:T(8,128)S(1)} %bitcast.2), custom_call_target="tpu_custom_call" | custom-call | tf_op jit(solution)/shard_map/panel_step/pallas_call | solution.py:387
  112.6 0.7 copy.4
Async XLA Ops:
  0.0 2.2 %copy-start = (f32[1024,1024]{1,0:T(8,128)S(1)}, f32[1024,1024]{1,0:T(8,128)}, u32[]{:S(2)}) copy-start(f32[1024,1024]{1,0:T(8,128)} %param.3) | copy-start | bytes 12582916
  2.2 0.7 copy-start.1

commit v3 on v2

--- a/solution.py
+++ b/solution.py
@@ -11,6 +11,7 @@
 ROWS = 1024
 DEPTH = 1024
 HALF = 128
+LAG = 2
 NZ, NX, NC, NCOL = 8, 4, 2, 4
 WIDE = DEPTH + 128
 
@@ -89,10 +90,9 @@
         self.buf, self.sz, self.rz, self.sx, self.rx, self.sc, self.rc = buf, sz, rz, sx, rx, sc, rc
         _, self.r, _, self.z, self.x, self.core = place()
 
-    def along_z(self, source, d):
-        target = (self.z + d) % NZ
+    def along_z(self, source, target):
         block = self.buf.at[source, self.x, self.core]
-        return send(block, block, self.sz.at[d - 1], self.rz.at[source], {"row": target * 8 + self.x * 2 + self.core})
+        return send(block, block, self.sz.at[target], self.rz.at[source], {"row": target * 8 + self.x * 2 + self.core})
 
     def along_x(self, source, e):
         target = (self.x + e) % NX
@@ -109,40 +109,72 @@
         block = self.buf.at[source, :, core]
         return send(block, block, self.sc.at[source], self.rc.at[source], {"row": self.r + 1 - 2 * self.core})
 
-    def run(self):
+    def outward(self, visit):
+        def ring(k, carry):
+            @pl.when(self.z >= k)
+            def _():
+                visit(self.z - k)
+
+            @pl.when(self.z + k < NZ)
+            def _():
+                visit(self.z + k)
+
+            return carry
+
+        lax.fori_loop(1, NZ, ring, 0)
+
+    def run(self, middle=None, arrived=None):
         z = self.z
-        for d in range(1, NZ):
-            self.along_z(z, d).start()
-        for e in range(1, NX):
-            self.along_x(z, e).start()
-
-        def forward(d, carry):
-            source = (z + NZ - d) % NZ
-            self.along_z(source, 1).wait_recv()
+        self.outward(lambda target: self.along_z(z, target).start())
+
+        def spread_x(source):
             for e in range(1, NX):
                 self.along_x(source, e).start()
-            return carry
-
-        lax.fori_loop(1, NZ, forward, 0)
-
-        def swap(d, carry):
-            source = (z + NZ - d) % NZ
+
+        def forward(source):
+            self.along_z(source, z).wait_recv()
+            spread_x(source)
+
+        def swap(source):
             for e in range(1, NX):
                 self.from_x(source, e).wait_recv()
             self.across(source, self.core).start()
+
+        def arrive(source):
+            self.across(source, 1 - self.core).wait_recv()
+            if arrived is not None:
+                arrived(source)
+
+        spread_x(z)
+
+        def ring(k, carry):
+            for act, j in ((forward, k), (swap, k - LAG)):
+                @pl.when((j > 0) & (z >= j))
+                def _():
+                    act(z - j)
+
+                @pl.when((j > 0) & (z + j < NZ))
+                def _():
+                    act(z + j)
+
+                if act is swap:
+                    @pl.when(j == 0)
+                    def _():
+                        act(z)
+
+            if middle is not None:
+                @pl.when(k == NZ - 1)
+                def _():
+                    middle()
+
             return carry
 
-        lax.fori_loop(0, NZ, swap, 0)
-
-        def arrive(source, carry):
-            self.across(source, 1 - self.core).wait_recv()
-            return carry
-
-        lax.fori_loop(0, NZ, arrive, 0)
+        lax.fori_loop(1, NZ + LAG, ring, 0)
+        arrive(z)
+        self.outward(arrive)
 
     def finish(self):
-        for d in range(1, NZ):
-            self.along_z(self.z, d).wait_send()
+        self.outward(lambda target: self.along_z(self.z, target).wait_send())
 
         def drain(source, carry):
             for e in range(1, NX):
@@ -155,7 +187,7 @@
 
 def gather_sems():
     dma = pltpu.SemaphoreType.DMA
-    return [dma((NZ - 1,)), dma((NZ,)), dma((NZ, NX - 1)), dma((NZ, NX)), dma((NZ,)), dma((NZ,))]
+    return [dma((NZ,)), dma((NZ,)), dma((NZ, NX - 1)), dma((NZ, NX)), dma((NZ,)), dma((NZ,))]
 
 
 def greet():
@@ -168,7 +200,7 @@
     peers += [{"gen": 1 - h, "col": (c + e) % NCOL} for e in range(NCOL)]
     for peer in peers:
         pl.semaphore_signal(barrier, inc=1, device_id=peer, device_id_type=MESH)
-    pl.semaphore_wait(barrier, len(peers))
+    return lambda: pl.semaphore_wait(barrier, len(peers))
 
 
 def halves(x):
@@ -185,19 +217,23 @@
 
 
 def step_kernel(
-    coords, factor, out, fv, pan, high, low, u, dgat, dy, dg, ybuf, gout, gbuf, marks, points, upd,
+    coords, factor, out, place_ref, fv, fhigh, flow, pan, high, low, u, dgat, dall, dsmall, dy, dg, ybuf, gout, gbuf, marks, points, upd,
     work, tile, inv, linv, xs, xt, local, sdy, rdy, sdg, rdg, sy, ry, sg, rg, sx, rx, *sems,
 ):
     h, r, c, z, x, core = place()
     f32 = jnp.float32
     load = pltpu.make_async_copy(factor, fv, local.at[0])
     rows = pltpu.make_async_copy(factor.at[0, 0, pl.ds(0, PAN), :], pan.at[z, x, core, :, pl.ds(0, DEPTH)], local.at[1])
+    where = pltpu.make_async_copy(coords, place_ref, local.at[3])
+    where.start()
     rows.start()
     load.start()
+    greeted = greet()
+    where.wait()
 
     sub = lax.broadcasted_iota(jnp.int32, (PAN, 128), 0)
     lane = lax.broadcasted_iota(jnp.int32, (PAN, 128), 1)
-    start = coords[:, :128].astype(f32) / GRID
+    start = place_ref[:, :128].astype(f32) / GRID
     mark = jnp.zeros((PAN, 128), f32)
     own_x, own_y = mark, mark
     for j in range(PAN):
@@ -210,16 +246,27 @@
     marks[...] = mark
     tag = pltpu.make_async_copy(marks, pan.at[z, x, core, :, pl.ds(DEPTH, 128)], local.at[2])
     tag.start()
-    greet()
+    load.wait()
+
+    def split(i, carry):
+        fhigh[i], flow[i] = halves(fv[i])
+        return carry
+
+    lax.fori_loop(0, 4, split, 0)
     rows.wait()
     tag.wait()
+    greeted()
     first = Gather(pan, *sems[:6])
     second = Gather(dgat, *sems[6:])
-    first.run()
-    load.wait()
+
+    def arrived(source):
+        at = pl.ds(pl.multiple_of(source * 64, 64), 64)
+        high[at, :], low[at, :] = halves(pan[source, :, :, :, :DEPTH].reshape(64, DEPTH))
+
+    first.run(arrived=arrived)
 
     def y_small(e):
-        return send(u.at[0, 0, pl.ds(0, PAN), :], dy.at[e - 1], sdy.at[e - 1], rdy.at[e - 1], {"col": (c + e) % NCOL})
+        return send(dsmall, dy.at[e - 1], sdy.at[e - 1], rdy.at[e - 1], {"col": (c + e) % NCOL})
 
     def y_large(s, e):
         part = (c + e) % NCOL
@@ -228,15 +275,26 @@
     gen_small = send(dy.at[NCOL - 1], dg, sdg.at[0], rdg.at[0], {"gen": 1 - h})
     gen_large = send(gout, gbuf, sg.at[0], rg.at[0], {"gen": 1 - h})
 
-    high[...], low[...] = halves(pan[:, :, :, :, :DEPTH].reshape(B, DEPTH))
+    def tile_of(i):
+        return (z // 2 + i) % 4
 
     def multiply(s):
-        a = halves(fv[:, s].reshape(4 * HALF, DEPTH))
+        a = [part[:, s].reshape(4 * HALF, DEPTH) for part in (fhigh, flow)]
         u[:, s] = three(a, (high[...], low[...])).reshape(4, HALF, B)
 
+    top = [part[0, 0, :16] for part in (fhigh, flow)]
+    rows8 = three(top, (high[...], low[...]))[:PAN]
+    for q in range(4):
+        dall[q] = rows8[:, 128 * q : 128 * q + 128]
+    for i in range(3):
+        dsmall[i] = dall[tile_of(i)]
+    for e in range(1, NCOL):
+        y_small(e).start()
     multiply(0)
     for e in range(1, NCOL):
-        y_small(e).start()
+        y_small(e).wait_recv()
+    dy[NCOL - 1] = dsmall[...] + dy[0] + dy[1] + dy[2]
+    gen_small.start()
 
     @pl.when(h == 1)
     def _():
@@ -244,11 +302,6 @@
             y_large(0, e).start()
 
     multiply(1)
-
-    for e in range(1, NCOL):
-        y_small(e).wait_recv()
-    dy[NCOL - 1] = u[0, 0, :PAN, :] + dy[0] + dy[1] + dy[2]
-    gen_small.start()
 
     @pl.when(h == 0)
     def _():
@@ -263,40 +316,49 @@
         total = grouped[q, 0]
         for i in range(1, 16):
             total = total + grouped[q, i]
-        points[:, 128 * q : 128 * q + 128] = total
+        points[q] = total
     kern = []
+    for i in range(3):
+        marked = points[tile_of(i)]
+        same = jnp.where(lane + 128 * tile_of(i) == sub + PAN * r, f32(nugget_term), f32(0))
+        kern.append(matern(own_x - marked[0:1], own_y - marked[1:2]) + same)
+    here = pl.ds(pl.multiple_of((c * 2 + h) * HALF, HALF), HALF)
+    mx = jnp.broadcast_to(place_ref[0:1, here].astype(f32) / GRID, (HALF, HALF)).T
+    my = jnp.broadcast_to(place_ref[1:2, here].astype(f32) / GRID, (HALF, HALF)).T
+    isub = lax.broadcasted_iota(jnp.int32, (HALF, 128), 0) + (c * 2 + h) * HALF
+    ilane = lax.broadcasted_iota(jnp.int32, (HALF, 128), 1)
     for q in range(4):
         at = slice(128 * q, 128 * q + 128)
-        same = jnp.where(lane + 128 * q == sub + PAN * r, f32(nugget_term), f32(0))
-        kern.append(matern(own_x - points[0:1, at], own_y - points[1:2, at]) + same)
+        same = (isub < PAN) & (ilane + 128 * q == isub + PAN * r)
+        k = matern(mx - points[q, 0:1], my - points[q, 1:2]) + jnp.where(same, f32(nugget_term), f32(0))
+        upd[:, at] = k
+    linv[...] = jnp.zeros((B, B), f32)
     gen_small.wait_recv()
-    for q in range(4):
-        at = slice(128 * q, 128 * q + 128)
-        dgat[z, x, core, :, at] = kern[q] - (dy[NCOL - 1, :, at] + dg[:, at])
-    second.run()
-    work[...] = dgat[...].reshape(B, B)
-
-    for e in range(1, NCOL):
-        y_large(1 - h, e).wait_recv()
-    gout[...] = u[c, 1 - h] + ybuf[1 - h, 0] + ybuf[1 - h, 1] + ybuf[1 - h, 2]
-    gen_large.start()
-
-    linv[...] = jnp.zeros((B, B), f32)
+    for i in range(3):
+        dgat[z, x, core, i] = kern[i] - (dy[NCOL - 1, i] + dg[i])
+
+    def pass_on():
+        for e in range(1, NCOL):
+            y_large(1 - h, e).wait_recv()
+        gout[...] = u[c, 1 - h] + ybuf[1 - h, 0] + ybuf[1 - h, 1] + ybuf[1 - h, 2]
+        gen_large.start()
+
+    second.run(middle=pass_on)
+    for t, i in ((0, 0), (0, 1), (0, 2), (1, 0), (1, 1), (1, 2), (2, 0), (2, 1), (3, 0), (3, 1)):
+        block = dgat[2 * t : 2 * t + 2, :, :, i].reshape(128, 128)
+        if t + i == 4:
+            block, row, col = block.T, 0, 3
+        else:
+            row, col = t, t + i
+        work[128 * row : 128 * row + 128, 128 * col : 128 * col + 128] = block
 
     def combine():
         for e in range(1, NCOL):
             y_large(h, e).wait_recv()
-        here = pl.ds(pl.multiple_of((c * 2 + h) * HALF, HALF), HALF)
-        mx = jnp.broadcast_to(coords[0:1, here].astype(f32) / GRID, (HALF, HALF)).T
-        my = jnp.broadcast_to(coords[1:2, here].astype(f32) / GRID, (HALF, HALF)).T
-        isub = lax.broadcasted_iota(jnp.int32, (HALF, 128), 0) + (c * 2 + h) * HALF
-        ilane = lax.broadcasted_iota(jnp.int32, (HALF, 128), 1)
         for q in range(4):
             at = slice(128 * q, 128 * q + 128)
-            same = (isub < PAN) & (ilane + 128 * q == isub + PAN * r)
-            k = matern(mx - points[0:1, at], my - points[1:2, at]) + jnp.where(same, f32(nugget_term), f32(0))
             part = u[c, h, :, at] + ybuf[h, 0, :, at] + ybuf[h, 1, :, at] + ybuf[h, 2, :, at]
-            upd[:, at] = k - part
+            upd[:, at] = upd[:, at] - part
 
     def settle():
         gen_large.wait_recv()
@@ -340,7 +402,10 @@
                 linv[lo:hi, lo:hi] = t
                 if v < 3:
                     p = dotf(t, work[lo:hi, hi:], ((1,), (0,)))
-                    work[hi:, hi:] = work[hi:, hi:] - dotf(p, p, ((0,), (0,)))
+                    for w in range(v + 1, 4):
+                        at = slice(128 * w, 128 * w + 128)
+                        left = slice(128 * w - hi, 128 * w + 128 - hi)
+                        work[at, 128 * w :] = work[at, 128 * w :] - dotf(p[:, left], p[:, 128 * w - hi :], ((0,), (0,)))
                     linv[hi:, :hi] = linv[hi:, :hi] - dotf(p, linv[lo:hi, :hi], ((0,), (0,)))
                 if v == 1:
                     combine()
@@ -387,22 +452,27 @@
     solved = pl.pallas_call(
         step_kernel,
         out_shape=jax.ShapeDtypeStruct((B // 8, ROWS), jnp.float32),
-        in_specs=[vmem, pl.BlockSpec(memory_space=pl.ANY)],
+        in_specs=[pl.BlockSpec(memory_space=pltpu.HBM)] * 2,
         out_specs=vmem,
         scratch_shapes=[
+            room(2, ROWS, dtype=jnp.int32),
             room(4, 2, HALF, DEPTH),
+            room(4, 2, HALF, DEPTH, dtype=jnp.bfloat16),
+            room(4, 2, HALF, DEPTH, dtype=jnp.bfloat16),
             room(NZ, NX, NC, PAN, WIDE),
             room(B, DEPTH, dtype=jnp.bfloat16),
             room(B, DEPTH, dtype=jnp.bfloat16),
             room(4, 2, HALF, B),
-            room(NZ, NX, NC, PAN, B),
-            room(NCOL, PAN, B),
-            room(PAN, B),
+            room(NZ, NX, NC, 3, PAN, 128),
+            room(4, PAN, 128),
+            room(3, PAN, 128),
+            room(NCOL, 3, PAN, 128),
+            room(3, PAN, 128),
             room(2, NCOL - 1, HALF, B),
             room(HALF, B),
             room(HALF, B),
             room(PAN, 128),
-            room(PAN, B),
+            room(4, PAN, 128),
             room(HALF, B),
             room(B, B),
             room(128, 128),
@@ -410,12 +480,12 @@
             room(B, B),
             room(2 * NCOL, B // 8, HALF),
             room(2 * NCOL, B // 8, HALF),
-            dma((3,)), dma((3,)), dma((3,)), dma((1,)), dma((1,)), dma((2, 3)), dma((2, 3)),
+            dma((4,)), dma((3,)), dma((3,)), dma((1,)), dma((1,)), dma((2, 3)), dma((2, 3)),
             dma((1,)), dma((1,)), dma((8,)), dma((8,)),
             *gather_sems(), *gather_sems(),
         ],
         compiler_params=pltpu.CompilerParams(
-            collective_id=0, has_side_effects=True, vmem_limit_bytes=48 << 20
+            collective_id=0, has_side_effects=True, vmem_limit_bytes=60 << 20
         ),
         name="panel_step",
     )(coords, factor.reshape(4, 2, HALF, DEPTH))

time: 115 us -> 110 us (0.957); the launches traced: 113 us -> 110 us
  Pallas kernels: 110 us -> 108 us
  local copies, waits for them, and re-layouts: 3.59 us -> 1.67 us
    unnamed x5 -> x1, local copies, waits for them, and re-layouts: 3.59 us -> 1.67 us
    pallas_call x1, Pallas kernels: 110 us -> 108 us  [shards(): pl.pallas_call(step_kernel, out_shape=jax.ShapeDtypeStruct((B // 8, ROWS)...]
where the time goes in v3:
time: 110 us
  Pallas kernels  108 us (98%)
  local copies, waits for them, and re-layouts  1.67 us (2%)
    pallas_call x1, Pallas kernels, shards(): pl.pallas_call(step_kernel, out_shape=jax.ShapeDtypeStruct((B // 8, ROWS)...  108 us

profile of v3, /device:TPU:1, one launch (start us, length us, event | category | flops | bytes accessed | tf_op | source)
XLA Modules:
  0.0 110.1 jit_solution(14188142190069737142)
XLA Ops:
  0.0 108.4 %panel_step.1 = f32[64,1024]{1,0:T(8,128)} custom-call(s32[2,1024]{1,0:T(2,128)} %coords.1, f32[4,2,128,1024]{3,2,1,0:T(8,128)} %bitcast.2), custom_call_target="tpu_custom_call" | custom-call | tf_op jit(solution)/shard_map/panel_step/pallas_call | solution.py:452
  108.4 1.7 %copy.4 = f32[1024,64]{0,1:T(8,128)} copy(f32[1024,64]{0,1:T(8,128)} %bitcast.3) | data formatting | bytes 524288

commit v4 on v3

--- a/solution.py
+++ b/solution.py
@@ -61,7 +61,11 @@
         ua = [spread(a[b], k) for k in range(8)]
         ut = [spread(t[b], k) for k in range(8)]
         out_ref[8 * b : 8 * b + 8, :] = t[b] * lax.rsqrt(scale)
-        for i in range(b + 1, 16):
+        inverse_pivots = jnp.ones((8, 128), jnp.float32)
+        for k in range(8):
+            inverse_pivots = jnp.where(sub == k, recip[k], inverse_pivots)
+        scaled = a[b] * inverse_pivots
+        for i in range(b + 1, min(b + 1 + 2, 16)):
             c = [jnp.broadcast_to(a[i][:, 8 * b + k : 8 * b + k + 1], (8, 128)) for k in range(8)]
             da = dt = None
             for k in range(8):
@@ -72,8 +76,18 @@
                 dt = m * ut[k] if dt is None else dt + m * ut[k]
             a[i] = a[i] - da
             t[i] = t[i] - dt
-
-
+        if b + 1 + 2 < 16:
+            hi = scaled.astype(jnp.bfloat16).astype(jnp.float32); r1 = scaled - hi
+            mi = r1.astype(jnp.bfloat16).astype(jnp.float32); lo = r1 - mi
+            both = jnp.concatenate([a[b], t[b]], axis=1)
+            bh = both.astype(jnp.bfloat16).astype(jnp.float32); r2 = both - bh
+            bm = r2.astype(jnp.bfloat16).astype(jnp.float32); bl = r2 - bm
+            lhs = jnp.concatenate([hi, hi, mi, hi, lo, mi, hi, hi], axis=0).astype(jnp.bfloat16)
+            rhs = jnp.concatenate([bh, bm, bh, bl, bh, bm, 0 * bh, 0 * bh], axis=0).astype(jnp.bfloat16)
+            delta = lax.dot_general(lhs, rhs, (((0,), (0,)), ((), ())), preferred_element_type=jnp.float32)
+            for i in range(b + 1 + 2, 16):
+                a[i] = a[i] - delta[8 * i : 8 * i + 8, :128]
+                t[i] = t[i] - delta[8 * i : 8 * i + 8, 128:]
 def place():
     h, r, c = lax.axis_index("gen"), lax.axis_index("row"), lax.axis_index("col")
     return h, r, c, r // 8, (r // 2) % 4, r % 2
@@ -86,13 +100,9 @@
 
 
 class Gather:
-    def __init__(self, buf, sz, rz, sx, rx, sc, rc):
-        self.buf, self.sz, self.rz, self.sx, self.rx, self.sc, self.rc = buf, sz, rz, sx, rx, sc, rc
+    def __init__(self, buf, sx, rx, sc, rc):
+        self.buf, self.sx, self.rx, self.sc, self.rc = buf, sx, rx, sc, rc
         _, self.r, _, self.z, self.x, self.core = place()
-
-    def along_z(self, source, target):
-        block = self.buf.at[source, self.x, self.core]
-        return send(block, block, self.sz.at[target], self.rz.at[source], {"row": target * 8 + self.x * 2 + self.core})
 
     def along_x(self, source, e):
         target = (self.x + e) % NX
@@ -109,31 +119,13 @@
         block = self.buf.at[source, :, core]
         return send(block, block, self.sc.at[source], self.rc.at[source], {"row": self.r + 1 - 2 * self.core})
 
-    def outward(self, visit):
-        def ring(k, carry):
-            @pl.when(self.z >= k)
-            def _():
-                visit(self.z - k)
-
-            @pl.when(self.z + k < NZ)
-            def _():
-                visit(self.z + k)
-
-            return carry
-
-        lax.fori_loop(1, NZ, ring, 0)
-
-    def run(self, middle=None, arrived=None):
+    def run(self, away, fetch, aside, arrived=None):
         z = self.z
-        self.outward(lambda target: self.along_z(z, target).start())
-
-        def spread_x(source):
+
+        def forward(source):
+            fetch(source)
             for e in range(1, NX):
                 self.along_x(source, e).start()
-
-        def forward(source):
-            self.along_z(source, z).wait_recv()
-            spread_x(source)
 
         def swap(source):
             for e in range(1, NX):
@@ -145,37 +137,32 @@
             if arrived is not None:
                 arrived(source)
 
-        spread_x(z)
+        def visit(act, k):
+            d = away(k)
+            inside = (k >= 0) & (k < NZ)
+
+            @pl.when(inside & (z >= d))
+            def _():
+                act(z - d)
+
+            @pl.when(inside & (d > 0) & (z + d < NZ))
+            def _():
+                act(z + d)
 
         def ring(k, carry):
-            for act, j in ((forward, k), (swap, k - LAG)):
-                @pl.when((j > 0) & (z >= j))
-                def _():
-                    act(z - j)
-
-                @pl.when((j > 0) & (z + j < NZ))
-                def _():
-                    act(z + j)
-
-                if act is swap:
-                    @pl.when(j == 0)
-                    def _():
-                        act(z)
-
-            if middle is not None:
-                @pl.when(k == NZ - 1)
-                def _():
-                    middle()
-
+            visit(forward, k)
+            aside(k)
+            visit(swap, k - LAG)
             return carry
 
-        lax.fori_loop(1, NZ + LAG, ring, 0)
-        arrive(z)
-        self.outward(arrive)
+        def last(k, carry):
+            visit(arrive, k)
+            return carry
+
+        lax.fori_loop(0, NZ + LAG, ring, 0)
+        lax.fori_loop(0, NZ, last, 0)
 
     def finish(self):
-        self.outward(lambda target: self.along_z(self.z, target).wait_send())
-
         def drain(source, carry):
             for e in range(1, NX):
                 self.along_x(source, e).wait_send()
@@ -187,7 +174,7 @@
 
 def gather_sems():
     dma = pltpu.SemaphoreType.DMA
-    return [dma((NZ,)), dma((NZ,)), dma((NZ, NX - 1)), dma((NZ, NX)), dma((NZ,)), dma((NZ,))]
+    return [dma((NZ, NX - 1)), dma((NZ, NX)), dma((NZ,)), dma((NZ,))]
 
 
 def greet():
@@ -198,6 +185,7 @@
     peers += [{"row": r + 1 - 2 * core}]
     peers += [{"col": (c + e) % NCOL} for e in range(1, NCOL)]
     peers += [{"gen": 1 - h, "col": (c + e) % NCOL} for e in range(NCOL)]
+    peers += [{"gen": 1 - h, "row": (z + d) % NZ * 8 + x * 2 + core} for d in range(1, NZ)]
     for peer in peers:
         pl.semaphore_signal(barrier, inc=1, device_id=peer, device_id_type=MESH)
     return lambda: pl.semaphore_wait(barrier, len(peers))
@@ -217,8 +205,8 @@
 
 
 def step_kernel(
-    coords, factor, out, place_ref, fv, fhigh, flow, pan, high, low, u, dgat, dall, dsmall, dy, dg, ybuf, gout, gbuf, marks, points, upd,
-    work, tile, inv, linv, xs, xt, local, sdy, rdy, sdg, rdg, sy, ry, sg, rg, sx, rx, *sems,
+    coords, factor, out, place_ref, fv, fhigh, flow, pan, high, low, u, dgat, dall, dsmall, dy, dpart, ybuf, gout, gbuf, points, upd,
+    work, tile, inv, linv, xs, xt, local, sz, rz, sdy, rdy, sdg, rdg, sy, ry, sg, rg, sx, rx, *sems,
 ):
     h, r, c, z, x, core = place()
     f32 = jnp.float32
@@ -243,27 +231,49 @@
         own_y = jnp.where(sub == j, py, own_y)
         both = jnp.where(sub == 0, px, jnp.where(sub == 1, py, 0.0))
         mark = jnp.where(lane == (r % 16) * PAN + j, both, mark)
-    marks[...] = mark
-    tag = pltpu.make_async_copy(marks, pan.at[z, x, core, :, pl.ds(DEPTH, 128)], local.at[2])
-    tag.start()
+    pan[z, x, core, :, DEPTH:] = mark
+    rows.wait()
+    greeted()
+
+    first = Gather(pan, *sems[:4])
+    second = Gather(dgat, *sems[4:])
+
+    def panel_copy(source, target):
+        block = pan.at[source, x, core]
+        return send(block, block, sz.at[target], rz.at[source], {"row": target * 8 + x * 2 + core})
+
+    def panel_each(act):
+        def ring(k, carry):
+            @pl.when(z >= k)
+            def _():
+                act(panel_copy(z, z - k))
+
+            @pl.when(z + k < NZ)
+            def _():
+                act(panel_copy(z, z + k))
+
+            return carry
+
+        lax.fori_loop(1, NZ, ring, 0)
+
+    panel_each(lambda copy: copy.start())
     load.wait()
 
-    def split(i, carry):
-        fhigh[i], flow[i] = halves(fv[i])
-        return carry
-
-    lax.fori_loop(0, 4, split, 0)
-    rows.wait()
-    tag.wait()
-    greeted()
-    first = Gather(pan, *sems[:6])
-    second = Gather(dgat, *sems[6:])
+    def panel_fetch(source):
+        @pl.when(source != z)
+        def _():
+            panel_copy(source, z).wait_recv()
+
+    def split(k):
+        @pl.when(k < 8)
+        def _():
+            fhigh[k // 2, k % 2], flow[k // 2, k % 2] = halves(fv[k // 2, k % 2])
 
     def arrived(source):
         at = pl.ds(pl.multiple_of(source * 64, 64), 64)
         high[at, :], low[at, :] = halves(pan[source, :, :, :, :DEPTH].reshape(64, DEPTH))
 
-    first.run(arrived=arrived)
+    first.run(lambda k: k, panel_fetch, split, arrived)
 
     def y_small(e):
         return send(dsmall, dy.at[e - 1], sdy.at[e - 1], rdy.at[e - 1], {"col": (c + e) % NCOL})
@@ -272,7 +282,33 @@
         part = (c + e) % NCOL
         return send(u.at[part, s], ybuf.at[s, e - 1], sy.at[s, e - 1], ry.at[s, e - 1], {"col": part})
 
-    gen_small = send(dy.at[NCOL - 1], dg, sdg.at[0], rdg.at[0], {"gen": 1 - h})
+    ring_place = h * NZ + z
+
+    def part_copy(source, target):
+        block = dpart.at[source]
+        return send(block, block, sdg.at[target], rdg.at[source],
+                    {"gen": target // NZ, "row": target % NZ * 8 + x * 2 + core})
+
+    def part_each(act):
+        def ring(k, carry):
+            act(part_copy(ring_place, (ring_place + k) % (2 * NZ)))
+
+            @pl.when(k < NZ)
+            def _():
+                act(part_copy(ring_place, (ring_place + 2 * NZ - k) % (2 * NZ)))
+
+            return carry
+
+        lax.fori_loop(1, NZ + 1, ring, 0)
+
+    def part_fetch(source):
+        for g in range(2):
+            @pl.when(ring_place != g * NZ + source)
+            def _():
+                part_copy(g * NZ + source, ring_place).wait_recv()
+
+        dgat[source, x, core] = dpart[source] + dpart[NZ + source]
+
     gen_large = send(gout, gbuf, sg.at[0], rg.at[0], {"gen": 1 - h})
 
     def tile_of(i):
@@ -290,27 +326,6 @@
         dsmall[i] = dall[tile_of(i)]
     for e in range(1, NCOL):
         y_small(e).start()
-    multiply(0)
-    for e in range(1, NCOL):
-        y_small(e).wait_recv()
-    dy[NCOL - 1] = dsmall[...] + dy[0] + dy[1] + dy[2]
-    gen_small.start()
-
-    @pl.when(h == 1)
-    def _():
-        for e in range(1, NCOL):
-            y_large(0, e).start()
-
-    multiply(1)
-
-    @pl.when(h == 0)
-    def _():
-        for e in range(1, NCOL):
-            y_large(1, e).start()
-
-    for e in range(1, NCOL):
-        y_large(h, e).start()
-
     grouped = pan[:, :, :, :, DEPTH:].reshape(4, 16, PAN, 128)
     for q in range(4):
         total = grouped[q, 0]
@@ -322,6 +337,29 @@
         marked = points[tile_of(i)]
         same = jnp.where(lane + 128 * tile_of(i) == sub + PAN * r, f32(nugget_term), f32(0))
         kern.append(matern(own_x - marked[0:1], own_y - marked[1:2]) + same)
+    multiply(0)
+    for e in range(1, NCOL):
+        y_small(e).wait_recv()
+    for i in range(3):
+        total = dsmall[i] + dy[0, i] + dy[1, i] + dy[2, i]
+        dpart[ring_place, i] = jnp.where(h == 0, kern[i], 0.0) - total
+    part_each(lambda copy: copy.start())
+
+    @pl.when(h == 1)
+    def _():
+        for e in range(1, NCOL):
+            y_large(0, e).start()
+
+    multiply(1)
+
+    @pl.when(h == 0)
+    def _():
+        for e in range(1, NCOL):
+            y_large(1, e).start()
+
+    for e in range(1, NCOL):
+        y_large(h, e).start()
+
     here = pl.ds(pl.multiple_of((c * 2 + h) * HALF, HALF), HALF)
     mx = jnp.broadcast_to(place_ref[0:1, here].astype(f32) / GRID, (HALF, HALF)).T
     my = jnp.broadcast_to(place_ref[1:2, here].astype(f32) / GRID, (HALF, HALF)).T
@@ -333,17 +371,15 @@
         k = matern(mx - points[q, 0:1], my - points[q, 1:2]) + jnp.where(same, f32(nugget_term), f32(0))
         upd[:, at] = k
     linv[...] = jnp.zeros((B, B), f32)
-    gen_small.wait_recv()
-    for i in range(3):
-        dgat[z, x, core, i] = kern[i] - (dy[NCOL - 1, i] + dg[i])
-
-    def pass_on():
-        for e in range(1, NCOL):
-            y_large(1 - h, e).wait_recv()
-        gout[...] = u[c, 1 - h] + ybuf[1 - h, 0] + ybuf[1 - h, 1] + ybuf[1 - h, 2]
-        gen_large.start()
-
-    second.run(middle=pass_on)
+    def pass_on(k):
+        @pl.when(k == NZ - 1)
+        def _():
+            for e in range(1, NCOL):
+                y_large(1 - h, e).wait_recv()
+            gout[...] = u[c, 1 - h] + ybuf[1 - h, 0] + ybuf[1 - h, 1] + ybuf[1 - h, 2]
+            gen_large.start()
+
+    second.run(lambda k: NZ // 2 + ((k + 1) // 2) * (1 - 2 * (k % 2)), part_fetch, pass_on)
     for t, i in ((0, 0), (0, 1), (0, 2), (1, 0), (1, 1), (1, 2), (2, 0), (2, 1), (3, 0), (3, 1)):
         block = dgat[2 * t : 2 * t + 2, :, :, i].reshape(128, 128)
         if t + i == 4:
@@ -436,7 +472,8 @@
         y_small(e).wait_send()
         for s in range(2):
             y_large(s, e).wait_send()
-    gen_small.wait_send()
+    part_each(lambda copy: copy.wait_send())
+    panel_each(lambda copy: copy.wait_send())
     gen_large.wait_send()
     first.finish()
     second.finish()
@@ -466,12 +503,11 @@
             room(NZ, NX, NC, 3, PAN, 128),
             room(4, PAN, 128),
             room(3, PAN, 128),
-            room(NCOL, 3, PAN, 128),
-            room(3, PAN, 128),
+            room(NCOL - 1, 3, PAN, 128),
+            room(2 * NZ, 3, PAN, 128),
             room(2, NCOL - 1, HALF, B),
             room(HALF, B),
             room(HALF, B),
-            room(PAN, 128),
             room(4, PAN, 128),
             room(HALF, B),
             room(B, B),
@@ -480,7 +516,7 @@
             room(B, B),
             room(2 * NCOL, B // 8, HALF),
             room(2 * NCOL, B // 8, HALF),
-            dma((4,)), dma((3,)), dma((3,)), dma((1,)), dma((1,)), dma((2, 3)), dma((2, 3)),
+            dma((4,)), dma((NZ,)), dma((NZ,)), dma((3,)), dma((3,)), dma((2 * NZ,)), dma((2 * NZ,)), dma((2, 3)), dma((2, 3)),
             dma((1,)), dma((1,)), dma((8,)), dma((8,)),
             *gather_sems(), *gather_sems(),
         ],

time: 110 us -> 107 us (0.973)
  the two profiles are of different devices: /device:TPU:1 before, /device:TPU:120 now
where the time goes in v4:
time: 107 us
  Pallas kernels  106 us (99%)
  local copies, waits for them, and re-layouts  1.67 us (2%)
    pallas_call x1, Pallas kernels, shards(): pl.pallas_call(step_kernel, out_shape=jax.ShapeDtypeStruct((B // 8, ROWS)...  106 us

profile of v4, /device:TPU:120, one launch (start us, length us, event | category | flops | bytes accessed | tf_op | source)
XLA Modules:
  0.0 107.3 jit_solution(17826964630918694832)
XLA Ops:
  0.0 105.6 %panel_step.1 = f32[64,1024]{1,0:T(8,128)} custom-call(s32[2,1024]{1,0:T(2,128)} %coords.1, f32[4,2,128,1024]{3,2,1,0:T(8,128)} %bitcast.2), custom_call_target="tpu_custom_call" | custom-call | tf_op jit(solution)/shard_map/panel_step/pallas_call | solution.py:489
  105.7 1.7 %copy.4 = f32[1024,64]{0,1:T(8,128)} copy(f32[1024,64]{0,1:T(8,128)} %bitcast.3) | data formatting | bytes 524288

commit v5 on v4

--- a/solution.py
+++ b/solution.py
@@ -357,9 +357,6 @@
         for e in range(1, NCOL):
             y_large(1, e).start()
 
-    for e in range(1, NCOL):
-        y_large(h, e).start()
-
     here = pl.ds(pl.multiple_of((c * 2 + h) * HALF, HALF), HALF)
     mx = jnp.broadcast_to(place_ref[0:1, here].astype(f32) / GRID, (HALF, HALF)).T
     my = jnp.broadcast_to(place_ref[1:2, here].astype(f32) / GRID, (HALF, HALF)).T
@@ -378,6 +375,8 @@
                 y_large(1 - h, e).wait_recv()
             gout[...] = u[c, 1 - h] + ybuf[1 - h, 0] + ybuf[1 - h, 1] + ybuf[1 - h, 2]
             gen_large.start()
+            for e in range(1, NCOL):
+                y_large(h, e).start()
 
     second.run(lambda k: NZ // 2 + ((k + 1) // 2) * (1 - 2 * (k % 2)), part_fetch, pass_on)
     for t, i in ((0, 0), (0, 1), (0, 2), (1, 0), (1, 1), (1, 2), (2, 0), (2, 1), (3, 0), (3, 1)):
@@ -445,29 +444,13 @@
                     linv[hi:, :hi] = linv[hi:, :hi] - dotf(p, linv[lo:hi, :hi], ((0,), (0,)))
                 if v == 1:
                     combine()
-                if v == 2:
                     settle()
-                    for w in range(3):
-                        solve(w)
-                if v == 3:
-                    solve(3)
+                    solve(0)
+                if v:
+                    solve(v)
         return carry
 
     lax.fori_loop(0, 4, step, 0)
-
-    for g in range(2 * NCOL):
-        @pl.when(h * NCOL + c != g)
-        def _():
-            theirs = (g % NCOL) * 2 + g // NCOL
-            send(xs.at[g], xt.at[theirs], sx.at[g], rx.at[theirs], {"gen": g // NCOL, "col": g % NCOL}).wait_recv()
-
-    for i in range(2 * NCOL):
-        out[:, HALF * i : HALF * i + HALF] = xt[i]
-
-    for g in range(2 * NCOL):
-        @pl.when(h * NCOL + c != g)
-        def _():
-            deliver(g).wait_send()
     for e in range(1, NCOL):
         y_small(e).wait_send()
         for s in range(2):
@@ -477,6 +460,20 @@
     gen_large.wait_send()
     first.finish()
     second.finish()
+
+    for g in range(2 * NCOL):
+        @pl.when(h * NCOL + c != g)
+        def _():
+            theirs = (g % NCOL) * 2 + g // NCOL
+            send(xs.at[g], xt.at[theirs], sx.at[g], rx.at[theirs], {"gen": g // NCOL, "col": g % NCOL}).wait_recv()
+
+    for i in range(2 * NCOL):
+        out[:, HALF * i : HALF * i + HALF] = xt[i]
+
+    for g in range(2 * NCOL):
+        @pl.when(h * NCOL + c != g)
+        def _():
+            deliver(g).wait_send()
 
 
 def shards(coords, factor):

time: 107 us -> 106 us (level)
  the two profiles are of different devices: /device:TPU:120 before, /device:TPU:152 now
where the time goes in v5:
time: 106 us
  Pallas kernels  104 us (98%)
  local copies, waits for them, and re-layouts  1.67 us (2%)
    pallas_call x1, Pallas kernels, shards(): pl.pallas_call(step_kernel, out_shape=jax.ShapeDtypeStruct((B // 8, ROWS)...  104 us

profile of v5, /device:TPU:152, one launch (start us, length us, event | category | flops | bytes accessed | tf_op | source)
XLA Modules:
  0.0 106.1 jit_solution(15925987514775806419)
XLA Ops:
  0.0 104.4 %panel_step.1 = f32[64,1024]{1,0:T(8,128)} custom-call(s32[2,1024]{1,0:T(2,128)} %coords.1, f32[4,2,128,1024]{3,2,1,0:T(8,128)} %bitcast.2), custom_call_target="tpu_custom_call" | custom-call | tf_op jit(solution)/shard_map/panel_step/pallas_call | solution.py:486
  104.4 1.7 %copy.4 = f32[1024,64]{0,1:T(8,128)} copy(f32[1024,64]{0,1:T(8,128)} %bitcast.3) | data formatting | bytes 524288

commit v6 on v5

--- a/solution.py
+++ b/solution.py
@@ -206,17 +206,17 @@
 
 def step_kernel(
     coords, factor, out, place_ref, fv, fhigh, flow, pan, high, low, u, dgat, dall, dsmall, dy, dpart, ybuf, gout, gbuf, points, upd,
-    work, tile, inv, linv, xs, xt, local, sz, rz, sdy, rdy, sdg, rdg, sy, ry, sg, rg, sx, rx, *sems,
+    work, inv, linv, xs, xt, local, sz, rz, sdy, rdy, sdg, rdg, sy, ry, sg, rg, sx, rx, *sems,
 ):
     h, r, c, z, x, core = place()
     f32 = jnp.float32
     load = pltpu.make_async_copy(factor, fv, local.at[0])
     rows = pltpu.make_async_copy(factor.at[0, 0, pl.ds(0, PAN), :], pan.at[z, x, core, :, pl.ds(0, DEPTH)], local.at[1])
+    greeted = greet()
     where = pltpu.make_async_copy(coords, place_ref, local.at[3])
     where.start()
     rows.start()
     load.start()
-    greeted = greet()
     where.wait()
 
     sub = lax.broadcasted_iota(jnp.int32, (PAN, 128), 0)
@@ -421,36 +421,38 @@
             def _():
                 deliver(g).start()
 
-    def step(k, carry):
-        for v in range(4):
-            @pl.when(k == v)
-            def _():
-                tile[...] = work[128 * v : 128 * v + 128, 128 * v : 128 * v + 128]
-        inverse_factor(tile, inv)
-        for v in range(4):
-            @pl.when(k == v)
-            def _():
-                lo, hi = 128 * v, 128 * v + 128
-                t = inv[...]
-                if v:
-                    linv[lo:hi, :lo] = dotf(t, linv[lo:hi, :lo], ((1,), (0,)))
-                linv[lo:hi, lo:hi] = t
-                if v < 3:
-                    p = dotf(t, work[lo:hi, hi:], ((1,), (0,)))
-                    for w in range(v + 1, 4):
-                        at = slice(128 * w, 128 * w + 128)
-                        left = slice(128 * w - hi, 128 * w + 128 - hi)
-                        work[at, 128 * w :] = work[at, 128 * w :] - dotf(p[:, left], p[:, 128 * w - hi :], ((0,), (0,)))
-                    linv[hi:, :hi] = linv[hi:, :hi] - dotf(p, linv[lo:hi, :hi], ((0,), (0,)))
-                if v == 1:
-                    combine()
-                    settle()
-                    solve(0)
-                if v:
-                    solve(v)
-        return carry
-
-    lax.fori_loop(0, 4, step, 0)
+    later = None
+    for v in range(4):
+        lo, hi = 128 * v, 128 * v + 128
+        inverse_factor(work.at[lo:hi, lo:hi], inv.at[v])
+        if later is not None:
+            later()
+        t = inv[v]
+        if v < 3:
+            p = dotf(t, work[lo:hi, hi:], ((1,), (0,)))
+            near = slice(hi, hi + 128)
+            work[near, near] = work[near, near] - dotf(p[:, :128], p[:, :128], ((0,), (0,)))
+        if v:
+            linv[lo:hi, :lo] = dotf(t, linv[lo:hi, :lo], ((1,), (0,)))
+        linv[lo:hi, lo:hi] = t
+
+        def later(p=p, lo=lo, hi=hi):
+            for w in range(hi // 128, 4):
+                at = slice(128 * w, 128 * w + 128)
+                left = slice(128 * w - hi, 128 * w + 128 - hi)
+                first_col = max(128 * w, hi + 128)
+                if first_col < B and (w > hi // 128 or first_col > 128 * w):
+                    work[at, first_col:] = work[at, first_col:] - dotf(p[:, left], p[:, first_col - hi :], ((0,), (0,)))
+            if hi < B:
+                linv[hi:, :hi] = linv[hi:, :hi] - dotf(p, linv[lo:hi, :hi], ((0,), (0,)))
+
+        if v == 1:
+            combine()
+            settle()
+            solve(0)
+        if v:
+            solve(v)
+
     for e in range(1, NCOL):
         y_small(e).wait_send()
         for s in range(2):
@@ -508,8 +510,7 @@
             room(4, PAN, 128),
             room(HALF, B),
             room(B, B),
-            room(128, 128),
-            room(128, 128),
+            room(4, 128, 128),
             room(B, B),
             room(2 * NCOL, B // 8, HALF),
             room(2 * NCOL, B // 8, HALF),

time: 106 us -> 106 us (level)
  the two profiles are of different devices: /device:TPU:152 before, /device:TPU:376 now
where the time goes in v6:
time: 106 us
  Pallas kernels  104 us (98%)
  local copies, waits for them, and re-layouts  1.67 us (2%)
    pallas_call x1, Pallas kernels, shards(): pl.pallas_call(step_kernel, out_shape=jax.ShapeDtypeStruct((B // 8, ROWS)...  104 us

profile of v6, /device:TPU:376, one launch (start us, length us, event | category | flops | bytes accessed | tf_op | source)
XLA Modules:
  0.0 106.1 jit_solution(16519810739031810422)
XLA Ops:
  0.0 104.4 %panel_step.1 = f32[64,1024]{1,0:T(8,128)} custom-call(s32[2,1024]{1,0:T(2,128)} %coords.1, f32[4,2,128,1024]{3,2,1,0:T(8,128)} %bitcast.2), custom_call_target="tpu_custom_call" | custom-call | tf_op jit(solution)/shard_map/panel_step/pallas_call | solution.py:488
  104.4 1.7 %copy.4 = f32[1024,64]{0,1:T(8,128)} copy(f32[1024,64]{0,1:T(8,128)} %bitcast.3) | data formatting | bytes 524288

commit v7 on v5

--- a/solution.py
+++ b/solution.py
@@ -11,7 +11,6 @@
 ROWS = 1024
 DEPTH = 1024
 HALF = 128
-LAG = 2
 NZ, NX, NC, NCOL = 8, 4, 2, 4
 WIDE = DEPTH + 128
 
@@ -119,7 +118,7 @@
         block = self.buf.at[source, :, core]
         return send(block, block, self.sc.at[source], self.rc.at[source], {"row": self.r + 1 - 2 * self.core})
 
-    def run(self, away, fetch, aside, arrived=None):
+    def run(self, away, fetch, aside, arrived=None, lag=2):
         z = self.z
 
         def forward(source):
@@ -152,14 +151,14 @@
         def ring(k, carry):
             visit(forward, k)
             aside(k)
-            visit(swap, k - LAG)
+            visit(swap, k - lag)
             return carry
 
         def last(k, carry):
             visit(arrive, k)
             return carry
 
-        lax.fori_loop(0, NZ + LAG, ring, 0)
+        lax.fori_loop(0, NZ + lag, ring, 0)
         lax.fori_loop(0, NZ, last, 0)
 
     def finish(self):
@@ -212,11 +211,11 @@
     f32 = jnp.float32
     load = pltpu.make_async_copy(factor, fv, local.at[0])
     rows = pltpu.make_async_copy(factor.at[0, 0, pl.ds(0, PAN), :], pan.at[z, x, core, :, pl.ds(0, DEPTH)], local.at[1])
+    greeted = greet()
     where = pltpu.make_async_copy(coords, place_ref, local.at[3])
     where.start()
     rows.start()
     load.start()
-    greeted = greet()
     where.wait()
 
     sub = lax.broadcasted_iota(jnp.int32, (PAN, 128), 0)
@@ -378,7 +377,7 @@
             for e in range(1, NCOL):
                 y_large(h, e).start()
 
-    second.run(lambda k: NZ // 2 + ((k + 1) // 2) * (1 - 2 * (k % 2)), part_fetch, pass_on)
+    second.run(lambda k: NZ // 2 + ((k + 1) // 2) * (1 - 2 * (k % 2)), part_fetch, pass_on, lag=1)
     for t, i in ((0, 0), (0, 1), (0, 2), (1, 0), (1, 1), (1, 2), (2, 0), (2, 1), (3, 0), (3, 1)):
         block = dgat[2 * t : 2 * t + 2, :, :, i].reshape(128, 128)
         if t + i == 4:
@@ -518,7 +517,7 @@
             *gather_sems(), *gather_sems(),
         ],
         compiler_params=pltpu.CompilerParams(
-            collective_id=0, has_side_effects=True, vmem_limit_bytes=60 << 20
+            collective_id=0, has_side_effects=True, vmem_limit_bytes=53 << 20
         ),
         name="panel_step",
     )(coords, factor.reshape(4, 2, HALF, DEPTH))

time: 106 us -> 109 us (1.028)
  the two profiles are of different devices: /device:TPU:152 before, /device:TPU:121 now
where the time goes in v7:
time: 109 us
  Pallas kernels  108 us (99%)
  local copies, waits for them, and re-layouts  1.4 us (1%)
    pallas_call x1, Pallas kernels, shards(): pl.pallas_call(step_kernel, out_shape=jax.ShapeDtypeStruct((B // 8, ROWS)...  108 us

profile of v7, /device:TPU:121, one launch (start us, length us, event | category | flops | bytes accessed | tf_op | source)
XLA Modules:
  0.0 109.2 jit_solution(446947367321892206)
XLA Ops:
  0.0 0.0 copy-start
  0.0 0.7 copy-done
  0.7 107.8 %panel_step.1 = f32[64,1024]{1,0:T(8,128)S(1)} custom-call(s32[2,1024]{1,0:T(2,128)S(1)} %copy-done, f32[4,2,128,1024]{3,2,1,0:T(8,128)} %bitcast.3), custom_call_target="tpu_custom_call" | custom-call | tf_op jit(solution)/shard_map/panel_step/pallas_call | solution.py:485
  108.5 0.7 copy.4
Async XLA Ops:
  0.0 0.7 copy-start

commit v8 on v5

--- a/solution.py
+++ b/solution.py
@@ -124,7 +124,7 @@
 
         def forward(source):
             fetch(source)
-            for e in range(1, NX):
+            for e in (2, 1, 3):
                 self.along_x(source, e).start()
 
         def swap(source):
@@ -290,7 +290,8 @@
                     {"gen": target // NZ, "row": target % NZ * 8 + x * 2 + core})
 
     def part_each(act):
-        def ring(k, carry):
+        def ring(step, carry):
+            k = NZ + 1 - step
             act(part_copy(ring_place, (ring_place + k) % (2 * NZ)))
 
             @pl.when(k < NZ)
@@ -324,7 +325,7 @@
         dall[q] = rows8[:, 128 * q : 128 * q + 128]
     for i in range(3):
         dsmall[i] = dall[tile_of(i)]
-    for e in range(1, NCOL):
+    for e in (2, 1, 3):
         y_small(e).start()
     grouped = pan[:, :, :, :, DEPTH:].reshape(4, 16, PAN, 128)
     for q in range(4):

time: 106 us -> 106 us (level)
  the two profiles are of different devices: /device:TPU:152 before, /device:TPU:376 now
where the time goes in v8:
time: 106 us; the launch traced here: 105 us
  Pallas kernels  104 us (98%)
  local copies, waits for them, and re-layouts  1.67 us (2%)
    pallas_call x1, Pallas kernels, shards(): pl.pallas_call(step_kernel, out_shape=jax.ShapeDtypeStruct((B // 8, ROWS)...  104 us

profile of v8, /device:TPU:376, one launch (start us, length us, event | category | flops | bytes accessed | tf_op | source)
XLA Modules:
  0.0 105.4 jit_solution(1236156961028473383)
XLA Ops:
  0.0 103.7 %panel_step.1 = f32[64,1024]{1,0:T(8,128)} custom-call(s32[2,1024]{1,0:T(2,128)} %coords.1, f32[4,2,128,1024]{3,2,1,0:T(8,128)} %bitcast.2), custom_call_target="tpu_custom_call" | custom-call | tf_op jit(solution)/shard_map/panel_step/pallas_call | solution.py:487
  103.7 1.7 %copy.4 = f32[1024,64]{0,1:T(8,128)} copy(f32[1024,64]{0,1:T(8,128)} %bitcast.3) | data formatting | bytes 524288

commit v9 on v8

--- a/solution.py
+++ b/solution.py
@@ -243,7 +243,9 @@
         return send(block, block, sz.at[target], rz.at[source], {"row": target * 8 + x * 2 + core})
 
     def panel_each(act):
-        def ring(k, carry):
+        def ring(step, carry):
+            k = NZ - step
+
             @pl.when(z >= k)
             def _():
                 act(panel_copy(z, z - k))
@@ -273,7 +275,7 @@
         at = pl.ds(pl.multiple_of(source * 64, 64), 64)
         high[at, :], low[at, :] = halves(pan[source, :, :, :, :DEPTH].reshape(64, DEPTH))
 
-    first.run(lambda k: k, panel_fetch, split, arrived)
+    first.run(lambda k: (NZ - k) % NZ, panel_fetch, split, arrived)
 
     def y_small(e):
         return send(dsmall, dy.at[e - 1], sdy.at[e - 1], rdy.at[e - 1], {"col": (c + e) % NCOL})

time: 106 us -> 108 us (1.019)
  the two profiles are of different devices: /device:TPU:376 before, /device:TPU:1 now
where the time goes in v9:
time: 108 us; the launch traced here: 106 us
  Pallas kernels  105 us (97%)
  local copies, waits for them, and re-layouts  1.67 us (2%)
    pallas_call x1, Pallas kernels, shards(): pl.pallas_call(step_kernel, out_shape=jax.ShapeDtypeStruct((B // 8, ROWS)...  105 us

profile of v9, /device:TPU:1, one launch (start us, length us, event | category | flops | bytes accessed | tf_op | source)
XLA Modules:
  0.0 106.3 jit_solution(6542990773832629268)
XLA Ops:
  0.0 104.6 %panel_step.1 = f32[64,1024]{1,0:T(8,128)} custom-call(s32[2,1024]{1,0:T(2,128)} %coords.1, f32[4,2,128,1024]{3,2,1,0:T(8,128)} %bitcast.2), custom_call_target="tpu_custom_call" | custom-call | tf_op jit(solution)/shard_map/panel_step/pallas_call | solution.py:489
  104.6 1.7 %copy.4 = f32[1024,64]{0,1:T(8,128)} copy(f32[1024,64]{0,1:T(8,128)} %bitcast.3) | data formatting | bytes 524288
